TPU v7x, 256 devices: a whole 4x4x8 slice. The times are simulated.
256 devices in a mesh: rep: 4 (over y_lo, core), exp: 64 (over x, y_hi, z).
Axes of the slice: x: 4, y: 4 (y_hi: 2, y_lo: 2; y = y_hi * 2 + y_lo), z: 8, core: 2. Of those that a mesh axis runs over, the one named last changes fastest.
Arguments:
- attn_out: bfloat16 [32768, 2048], P(('rep', 'exp')), may hold values from -24 to 24
- resid: bfloat16 [32768, 1024], P(('rep', 'exp')), may hold values from -6 to 6
- out_grad: bfloat16 [32768, 1024], P(('rep', 'exp')), may hold values from -6 to 6
- gain: float32 [1024], replicated, may hold values from 0.5 to 1.5
- expert_ids: int32 [32768, 8], P(('rep', 'exp')), may hold values from 0 to 63, all different within a row; in each aligned block of 128 rows (0 to 127, 128 to 255, ...) at most 18 rows name the same one
- gate_vals: float32 [32768, 8], P(('rep', 'exp')), may hold values from 0.03 to 0.5
- w_gate: bfloat16 [64, 1024, 512], P('exp'), may hold values from -0.1875 to 0.1875
- w_up: bfloat16 [64, 1024, 512], P('exp'), may hold values from -0.1875 to 0.1875
- w_down: bfloat16 [64, 512, 1024], P('exp'), may hold values from -0.25 to 0.25
Outputs:
- d_resid: bfloat16 [32768, 1024], P(('rep', 'exp'))
- projection_grad: float32 [2048, 1024], P(('rep', 'exp'))
- gate_grad: float32 [64, 1024, 512], P('exp', None, 'rep')
- up_grad: float32 [64, 1024, 512], P('exp', None, 'rep')
- down_grad: float32 [64, 512, 1024], P('exp', None, 'rep')
Inputs may be any that keep to these rules, and one draw needn't show every extreme that they name: `expert_ids`: each row names 8 different experts. Among the rows of one device no expert is named more than 18 times, a bound that some block reaches.
All inputs are finite; a program needn't handle non-finite values.
Results may differ from a plain program's by a relative error of at most 0.0095.
Values may be sent and summed in bfloat16 or wider, within the bound.
No kernel may reach another device: no remote copies, remote signals or barrier semaphores. Data moves between devices by JAX's collectives and lax.ppermute only.
A program may use at most 128 MiB of HBM per device.

v0:
```python
import functools

import jax
import jax.numpy as jnp
from jax import lax
from jax.experimental import pallas as pl
from jax.experimental.pallas import tpu as pltpu
from jax.sharding import Mesh, PartitionSpec as P

epsilon = 1e-06
AXES = ("ylo", "core", "x", "yhi", "z")
RING = 8
PLANE = 8
TOP = 8
CAPACITY = 18
META = 128
NEAR = (0, -1, 1)
FAR = (-2, 2, -3, 3, 4)
bf16 = jnp.bfloat16
f32 = jnp.float32


def contract_rows(left, right):
    return lax.dot_general(left, right, (((0,), (0,)), ((), ())), preferred_element_type=f32)


def contract_last(left, right):
    return lax.dot_general(left, right, (((1,), (1,)), ((), ())), preferred_element_type=f32)


def shift_z(block, step):
    return lax.ppermute(block, "z", [(i, (i + step) % RING) for i in range(RING)])


def swap(block, axis):
    return lax.ppermute(block, axis, [(0, 1), (1, 0)])


def y_peer(step):
    pairs = []
    for y in range(4):
        to = (y + step) % 4
        pairs.append(((y % 2) * 2 + y // 2, (to % 2) * 2 + to // 2))
    return pairs


def ring_scatter(blocks):
    half = blocks[4].shape[1] // 2
    far = blocks[4].astype(bf16)
    got = shift_z(far[:, :half], 1).astype(f32)
    right = jnp.concatenate([blocks[3][:, :half] + got, blocks[3][:, half:]], axis=1)
    got = shift_z(far[:, half:], -1).astype(f32)
    left = jnp.concatenate([blocks[-3][:, :half], blocks[-3][:, half:] + got], axis=1)
    for d in (2, 1, 0):
        got_right = shift_z(right.astype(bf16), 1).astype(f32)
        got_left = shift_z(left.astype(bf16), -1).astype(f32)
        if d:
            right = blocks[d] + got_right
            left = blocks[-d] + got_left
    return blocks[0] + got_right + got_left


def enter_kernel(resid_ref, grad_ref, gain_ref, ids_ref, vals_ref, out_ref):
    tokens, feature = resid_ref.shape
    resid = resid_ref[...].astype(f32)
    inv_rms = lax.rsqrt(jnp.mean(resid * resid, axis=1, keepdims=True) + epsilon)
    out_ref[:, :feature] = (resid * inv_rms * gain_ref[...]).astype(bf16)
    out_ref[:, feature : 2 * feature] = grad_ref[...]
    vals = vals_ref[...]
    high = vals.astype(bf16).astype(f32)
    middle = (vals - high).astype(bf16).astype(f32)
    low = vals - high - middle
    rest = jnp.zeros((tokens, META - 4 * TOP), f32)
    meta = jnp.concatenate([ids_ref[...].astype(f32), high, middle, low, rest], axis=1)
    out_ref[:, 2 * feature :] = meta.astype(bf16)


def enter(resid, out_grad, gain, expert_ids, gate_vals):
    tokens, feature = resid.shape
    return pl.pallas_call(
        enter_kernel,
        out_shape=jax.ShapeDtypeStruct((tokens, 2 * feature + META), bf16),
    )(resid, out_grad, gain.reshape(1, feature), expert_ids, gate_vals)


def pick_kernel(layout, z_ref, *refs):
    pieces = sum(len(widths) for widths in layout)
    ins, out_ref, target_ref, held, gates = refs[:pieces], *refs[pieces:]
    rows, width = out_ref.shape[1:]
    half = width // 2
    tokens = ins[0].shape[0]

    @pl.when(pl.program_id(0) == 0)
    def _():
        own = lax.broadcasted_iota(jnp.int32, (PLANE, tokens), 0) * RING + z_ref[0]
        own = own.astype(f32)
        earlier = lax.broadcasted_iota(jnp.int32, (tokens, tokens), 0)
        earlier = earlier < lax.broadcasted_iota(jnp.int32, (tokens, tokens), 1)
        earlier = jnp.where(earlier, 1.0, 0.0).astype(bf16)
        at = 0
        for i, widths in enumerate(layout):
            lines = slice(i * tokens, (i + 1) * tokens)
            column = 0
            for piece in widths:
                ref = ins[at]
                data = piece
                if column + piece > width:
                    data = width - column
                    meta = ref[:, data:]
                held[lines, column : column + data] = ref[:, :data]
                column += data
                at += 1
            meta = meta.astype(f32).T
            value = meta[TOP : 2 * TOP] + meta[2 * TOP : 3 * TOP] + meta[3 * TOP : 4 * TOP]
            named = jnp.zeros((PLANE, tokens), f32)
            gate = jnp.zeros((PLANE, tokens), f32)
            for k in range(TOP):
                same = meta[k : k + 1] == own
                named = jnp.where(same, 1.0, named)
                gate = jnp.where(same, value[k : k + 1], gate)
            slot = jnp.dot(named.astype(bf16), earlier, preferred_element_type=f32)
            place = jnp.where(named > 0.5, slot + float(i * CAPACITY), -1.0)
            target_ref[:, lines] = place
            gates[:, lines] = gate

    e = pl.program_id(0)
    row_ids = lax.broadcasted_iota(jnp.int32, (rows, held.shape[0]), 0).astype(f32)
    hit = row_ids == target_ref[pl.ds(e, 1), :]
    gate = jnp.sum(jnp.where(hit, gates[pl.ds(e, 1), :], 0.0), axis=1, keepdims=True)
    onehot = jnp.where(hit, 1.0, 0.0).astype(bf16)
    picked = jnp.dot(onehot, held[:, :half], preferred_element_type=f32)
    out_ref[0, :, :half] = picked.astype(bf16)
    picked = jnp.dot(onehot, held[:, half:], preferred_element_type=f32)
    out_ref[0, :, half:] = (picked * gate).astype(bf16)


def pick_rows(z, blocks, width):
    count = len(blocks)
    tokens = blocks[0][0].shape[0]
    rows = -(-count * CAPACITY // 8) * 8
    flat = [piece for block in blocks for piece in block]
    layout = tuple(tuple(piece.shape[1] for piece in block) for block in blocks)
    whole = [pl.BlockSpec(piece.shape, lambda e, z: (0, 0)) for piece in flat]
    return pl.pallas_call(
        functools.partial(pick_kernel, layout),
        grid_spec=pltpu.PrefetchScalarGridSpec(
            num_scalar_prefetch=1,
            grid=(PLANE,),
            in_specs=whole,
            out_specs=[
                pl.BlockSpec((1, rows, width), lambda e, z: (e, 0, 0)),
                pl.BlockSpec((PLANE, count * tokens), lambda e, z: (0, 0)),
            ],
            scratch_shapes=[
                pltpu.VMEM((count * tokens, width), bf16),
                pltpu.VMEM((PLANE, count * tokens), f32),
            ],
        ),
        out_shape=[
            jax.ShapeDtypeStruct((PLANE, rows, width), bf16),
            jax.ShapeDtypeStruct((PLANE, count * tokens), f32),
        ],
        compiler_params=pltpu.CompilerParams(vmem_limit_bytes=24 << 20),
        cost_estimate=pl.CostEstimate(
            flops=2 * PLANE * rows * count * tokens * width,
            bytes_accessed=2 * width * (count * tokens + PLANE * rows),
            transcendentals=0,
        ),
    )(z.reshape(1), *flat)


def expert_kernel(got_ref, w_gate_ref, w_up_ref, w_down_ref, back_ref, slopes_ref, hidden_ref):
    feature = back_ref.shape[1]
    inner = hidden_ref.shape[1]
    rows_in, rows_grad = got_ref[:, :feature], got_ref[:, feature:]
    pre_gate = jnp.dot(rows_in, w_gate_ref[...], preferred_element_type=f32)
    pre_up = jnp.dot(rows_in, w_up_ref[...], preferred_element_type=f32)
    d_hidden = contract_last(rows_grad, w_down_ref[...])
    sigma = jax.nn.sigmoid(pre_gate)
    active = pre_gate * sigma
    hidden_ref[...] = (active * pre_up).astype(bf16)
    d_gate = (d_hidden * pre_up * (sigma * (1.0 + pre_gate * (1.0 - sigma)))).astype(bf16)
    d_up = (d_hidden * active).astype(bf16)
    for i in range(inner // 128):
        slopes_ref[:, 256 * i : 256 * i + 128] = d_gate[:, 128 * i : 128 * i + 128]
        slopes_ref[:, 256 * i + 128 : 256 * i + 256] = d_up[:, 128 * i : 128 * i + 128]
    back = contract_last(d_gate, w_gate_ref[...]) + contract_last(d_up, w_up_ref[...])
    back_ref[...] = back.astype(bf16)


def run_expert(got, w_gate, w_up, w_down, steps):
    total, width = got.shape
    feature, inner = w_gate.shape
    rows = total // steps
    return pl.pallas_call(
        expert_kernel,
        grid=(steps,),
        in_specs=[
            pl.BlockSpec((rows, width), lambda i: (i, 0)),
            pl.BlockSpec((feature, inner), lambda i: (0, 0)),
            pl.BlockSpec((feature, inner), lambda i: (0, 0)),
            pl.BlockSpec((inner, feature), lambda i: (0, 0)),
        ],
        out_specs=[
            pl.BlockSpec((rows, feature), lambda i: (i, 0)),
            pl.BlockSpec((rows, 2 * inner), lambda i: (i, 0)),
            pl.BlockSpec((rows, inner), lambda i: (i, 0)),
        ],
        out_shape=[
            jax.ShapeDtypeStruct((total, feature), bf16),
            jax.ShapeDtypeStruct((total, 2 * inner), bf16),
            jax.ShapeDtypeStruct((total, inner), bf16),
        ],
        compiler_params=pltpu.CompilerParams(vmem_limit_bytes=32 << 20),
        cost_estimate=pl.CostEstimate(
            flops=10 * total * feature * inner,
            bytes_accessed=2 * total * (width + feature + 3 * inner) + 6 * feature * inner,
            transcendentals=total * inner,
        ),
    )(got, w_gate, w_up, w_down)


def weights_kernel(core_ref, *refs):
    (x1, g1, s1, h1, x2, g2, s2, h2, other_ref, mine_ref) = refs
    feature = x1.shape[1]
    top = contract_rows(x1[...], s1[...]) + contract_rows(x2[...], s2[...])
    low = contract_rows(h1[...], g1[...]) + contract_rows(h2[...], g2[...])

    @pl.when(pl.program_id(0) < 2)
    def _():
        other_ref[0, :feature, :] = top.astype(bf16)
        other_ref[0, feature:, :] = low.astype(bf16)

    @pl.when(pl.program_id(0) >= 2)
    def _():
        mine_ref[0, :feature, :] = top
        mine_ref[0, feature:, :] = low


def weight_terms(core, near, far):
    specs, arrays, flops = [], [], 0
    for got, slopes, hidden in (near, far):
        rows, width = got.shape
        feature = width // 2
        inner = hidden.shape[1]
        share = feature // 4

        def block(s, core):
            return (s % 2) * 2 + jnp.where(s < 2, 1 - core[0], core[0])

        specs += [
            pl.BlockSpec((rows, feature), lambda s, core: (0, 0)),
            pl.BlockSpec((rows, share), lambda s, core: (0, 4 + block(s, core))),
            pl.BlockSpec((rows, share), lambda s, core: (0, block(s, core))),
            pl.BlockSpec((rows, inner), lambda s, core: (0, 0)),
        ]
        arrays += [got, got, slopes, hidden]
        flops += 2 * rows * feature * 3 * inner
    shape = (2, feature + inner, share)
    return pl.pallas_call(
        weights_kernel,
        grid_spec=pltpu.PrefetchScalarGridSpec(
            num_scalar_prefetch=1,
            grid=(4,),
            in_specs=specs,
            out_specs=[
                pl.BlockSpec((1,) + shape[1:], lambda s, core: (jnp.minimum(s, 1), 0, 0)),
                pl.BlockSpec((1,) + shape[1:], lambda s, core: (jnp.maximum(s - 2, 0), 0, 0)),
            ],
        ),
        out_shape=[jax.ShapeDtypeStruct(shape, bf16), jax.ShapeDtypeStruct(shape, f32)],
        compiler_params=pltpu.CompilerParams(vmem_limit_bytes=40 << 20),
        cost_estimate=pl.CostEstimate(flops=flops, bytes_accessed=16 << 20, transcendentals=0),
    )(core.reshape(1), *arrays)


def body(attn_out, resid, out_grad, gain, expert_ids, gate_vals, w_gate, w_up, w_down):
    tokens, feature = resid.shape
    z = lax.axis_index("z")
    core = lax.axis_index("core")
    ylo = lax.axis_index("ylo")
    yhi = lax.axis_index("yhi")
    w_gate, w_up, w_down = w_gate[0], w_up[0], w_down[0]

    mine = enter(resid, out_grad, gain, expert_ids, gate_vals)
    right, left = shift_z(mine, 1), shift_z(mine, -1)
    attn = attn_out.reshape(tokens, 2, 2, 4, 2, 64).transpose(1, 2, 4, 0, 3, 5).reshape(8, tokens, 256)
    attn = lax.all_to_all(attn, ("ylo", "core", "yhi"), split_axis=0, concat_axis=0, tiled=True)
    right, left, attn = lax.optimization_barrier((right, left, attn))
    gathered = {0: [mine], -1: [right], 1: [left]}
    for d in (2, 3):
        right, left = shift_z(right, 1), shift_z(left, -1)
        gathered[-d], gathered[d] = [right], [left]
    gathered[4] = [shift_z(right[:, :feature], 1), shift_z(left[:, feature:], -1)]

    def send(deltas):
        sent, target = pick_rows(z, [gathered[d] for d in deltas], 2 * feature)
        got = lax.all_to_all(sent, ("x", "yhi"), split_axis=0, concat_axis=0, tiled=True)
        return got.reshape(-1, 2 * feature), target

    def answer(got, steps):
        back, slopes, hidden = run_expert(got, w_gate, w_up, w_down, steps)
        back = back.reshape(PLANE, -1, feature)
        returned = lax.all_to_all(back, ("x", "yhi"), split_axis=0, concat_axis=0, tiled=True)
        return returned, (got, slopes, hidden)

    got_near, target_near = send(NEAR)
    got_far, target_far = send(FAR)
    returned_near, saved_near = answer(got_near, 2)
    returned_far, saved_far = answer(got_far, 3)
    other, own = weight_terms(core, saved_near, saved_far)
    returned_far, other, own = lax.optimization_barrier((returned_far, other, own))

    total = own + swap(other, "core").astype(f32)
    held = lax.dynamic_index_in_dim(total, ylo, 0, keepdims=False)
    other = lax.dynamic_index_in_dim(total, 1 - ylo, 0, keepdims=False)
    total = held + swap(other.astype(bf16), "ylo").astype(f32)
    half = total.shape[1] // 2
    gate_out, up_out, down_out = total[None, :feature, :half], total[None, :feature, half:], total[None, feature:]

    terms = {}
    for target, deltas, returned in ((target_near, NEAR, returned_near), (target_far, FAR, returned_far)):
        rows = returned.shape[1]
        pick = (jnp.arange(rows, dtype=jnp.int32).astype(f32)[None, :, None] == target[:, None, :]).astype(bf16)
        term = contract_rows(pick.reshape(PLANE * rows, -1), returned.reshape(PLANE * rows, feature))
        for i, d in enumerate(deltas):
            terms[d] = term[i * tokens : (i + 1) * tokens]
    d_moe = ring_scatter(terms)
    gain_f = gain[None, :]
    resid_f = resid.astype(f32)
    inv_rms = lax.rsqrt(jnp.mean(resid_f * resid_f, axis=1, keepdims=True) + epsilon)
    normed = resid_f * inv_rms
    d_norm = d_moe * gain_f
    inner = jnp.mean(d_norm * normed, axis=1, keepdims=True)
    d_resid = (out_grad.astype(f32) + inv_rms * (d_norm - normed * inner)).astype(bf16)

    attn = attn.reshape(2, 2, 2, tokens, 256)
    y = yhi * 2 + ylo
    pieces = []
    for step in (0, 1, 3, 2):
        block = d_resid if step == 0 else lax.ppermute(d_resid, ("ylo", "yhi"), y_peer(step))
        source = (y - step) % 4
        for crossed in (0, 1):
            piece = swap(block, "core") if crossed else block
            held = attn[source % 2, (core + crossed) % 2, source // 2]
            pieces.append((held, piece))
    part = contract_rows(
        jnp.concatenate([a for a, _ in pieces], axis=0), jnp.concatenate([b for _, b in pieces], axis=0)
    )
    part = part.astype(bf16).reshape(32, 8, feature)
    part = lax.all_to_all(part, ("x", "z"), split_axis=0, concat_axis=0, tiled=True)
    projection_grad = jnp.sum(part.astype(f32), axis=0)
    return (d_resid, projection_grad, gate_out, up_out, down_out)


def solution(mesh):
    whole = Mesh(mesh.devices.reshape(2, 2, 4, 2, RING), AXES)
    tok = P(AXES, None)
    exp = ("x", "yhi", "z")
    weights = P(exp, None, None)
    in_specs = (tok, tok, tok, P(), tok, tok, weights, weights, weights)
    grads = P(exp, None, ("ylo", "core"))
    out_specs = (tok, tok, grads, grads, grads)
    return jax.shard_map(body, mesh=whole, in_specs=in_specs, out_specs=out_specs, check_vma=False)
```

profile of v0, /device:TPU:1, one launch (start us, length us, event | category | flops | bytes accessed | tf_op | source)
XLA Modules:
  0.0 267.7 jit_solution(17574430991575887573)
XLA Ops:
  5.5 2.5 collective-permute-start
  8.0 3.9 %collective-permute-start.1 = (bf16[128,2176]{1,0:T(8,128)(2,1)}, bf16[128,2176]{1,0:T(8,128)(2,1)S(1)}, u32[]{:S(2)}, u32[]{:S(2)}) collective-permute-start(bf16[128,2176]{1,0:T(8,128)(2,1)} %shard_map.128.refs_0_), channel_id=1, source_target_pairs={{0,7},{1,0},{2,1},{3,2},{4,3},{5,4},{6,5},{7,6},{8,15},{9,8},{10,9... | collective-permute-start | bytes 1671176 | tf_op jit(solution)/shard_map/ppermute | solution.py:32
  13.3 14.7 %all_to_all.30 = bf16[8,128,256]{1,2,0:T(8,128)(2,1)} all-to-all(bf16[8,128,256]{1,2,0:T(8,128)(2,1)S(1)} %bitcast.69), channel_id=1, replica_groups=mesh['ylo'=2,'core'=2,'x'=4,'yhi'=2,'z'=8] {'ylo','core','yhi'}, dimensions={0} | all-to-all | bytes 1048576 | tf_op jit(solution)/shard_map/all_to_all | solution.py:288
  31.3 10.9 %collective-permute-done.3.refs_1_ = bf16[128,2176]{1,0:T(8,128)(2,1)S(1)} collective-permute-done((bf16[128,2176]{1,0:T(8,128)(2,1)S(1)}, bf16[128,2176]{1,0:T(8,128)(2,1)S(1)}, u32[]{:S(2)}, u32[]{:S(2)}) %collective-permute-start.3) | collective-permute-done | bytes 557088 | tf_op jit(solution)/shard_map/ppermute | solution.py:32
  42.2 3.0 %collective-permute-start.5 = (bf16[128,2176]{1,0:T(8,128)(2,1)S(1)}, bf16[128,2176]{1,0:T(8,128)(2,1)S(1)}, u32[]{:S(2)}, u32[]{:S(2)}) collective-permute-start(bf16[128,2176]{1,0:T(8,128)(2,1)S(1)} %collective-permute-done.3.refs_1_), channel_id=1, source_target_pairs={{0,7},{1,0},{2,1},{3,2},{4,3},{5,4},{6,5},{7,6},{8,15},{9,8},{10,9... | collective-permute-start | bytes 1671176 | tf_op jit(solution)/shard_map/ppermute | solution.py:32
  45.7 10.7 %collective-permute-done.5.refs_3_ = bf16[128,2176]{1,0:T(8,128)(2,1)S(1)} collective-permute-done((bf16[128,2176]{1,0:T(8,128)(2,1)S(1)}, bf16[128,2176]{1,0:T(8,128)(2,1)S(1)}, u32[]{:S(2)}, u32[]{:S(2)}) %collective-permute-start.5) | collective-permute-done | bytes 557088 | tf_op jit(solution)/shard_map/ppermute | solution.py:32
  56.4 3.5 %collective-permute-start.7 = (bf16[128,1152]{1,0:T(8,128)(2,1)S(1)}, bf16[128,1152]{1,0:T(8,128)(2,1)S(1)}, u32[]{:S(2)}, u32[]{:S(2)}) collective-permute-start(bf16[128,1152]{1,0:T(8,128)(2,1)S(1)} %slice.79), channel_id=1, source_target_pairs={{0,7},{1,0},{2,1},{3,2},{4,3},{5,4},{6,5},{7,6},{8,15},{9,8},{10,9... | collective-permute-start | bytes 884744 | tf_op jit(solution)/shard_map/ppermute | solution.py:32
  60.0 7.0 %collective-permute-done.6.refs_4_ = bf16[128,1024]{1,0:T(8,128)(2,1)S(1)} collective-permute-done((bf16[128,1024]{1,0:T(8,128)(2,1)S(1)}, bf16[128,1024]{1,0:T(8,128)(2,1)S(1)}, u32[]{:S(2)}, u32[]{:S(2)}) %collective-permute-start.6) | collective-permute-done | bytes 262176 | tf_op jit(solution)/shard_map/ppermute | solution.py:32
  67.0 5.1 %shard_map.131 = (bf16[8,96,2048]{2,1,0:T(8,128)(2,1)S(1)}, f32[8,640]{1,0:T(8,128)S(1)}) custom-call(s32[1]{0:T(128)} %bitcast.z_ref, bf16[128,2176]{1,0:T(8,128)(2,1)S(1)} %collective-permute-done.2.refs_0_, bf16[128,2176]{1,0:T(8,128)(2,1)S(1)} %collective-permute-done.3.refs_1_, bf16[128,2176]{1,0:T(8,128)(2,1)S(1)} %collective-permute-done.4.refs_2_, ...), custom_call_target="tpu_custom_call" | custom-call | flops 2013265920 | bytes 5767168 | tf_op jit(solution)/shard_map/pallas_call | solution.py:144
  73.8 4.0 %all-to-all-start.3 = ((bf16[8,96,2048]{2,1,0:T(8,128)(2,1)}), bf16[8,96,2048]{2,1,0:T(8,128)(2,1)S(1)}, u32[]{:S(2)}, u32[]{:S(2)}) async-start(bf16[8,96,2048]{2,1,0:T(8,128)(2,1)} %copy-done), calls=%async_computation.3 | async-start | bytes 6291456 | tf_op jit(solution)/shard_map/all_to_all | solution.py:298
  81.0 3.5 %shard_map.129 = (bf16[8,56,2048]{2,1,0:T(8,128)(2,1)S(1)}, f32[8,384]{1,0:T(8,128)S(1)}) custom-call(s32[1]{0:T(128)} %bitcast.z_ref, bf16[128,2176]{1,0:T(8,128)(2,1)S(1)} %copy-done.5, bf16[128,2176]{1,0:T(8,128)(2,1)S(1)} %copy-done.15, bf16[128,2176]{1,0:T(8,128)(2,1)S(1)} %copy-done.17), custom_call_target="tpu_custom_call" | custom-call | flops 704643072 | bytes 3407872 | tf_op jit(solution)/shard_map/pallas_call | solution.py:144
  85.8 35.0 %all-to-all-done.3 = bf16[8,96,2048]{2,1,0:T(8,128)(2,1)S(1)} async-done(((bf16[8,96,2048]{2,1,0:T(8,128)(2,1)}), bf16[8,96,2048]{2,1,0:T(8,128)(2,1)S(1)}, u32[]{:S(2)}, u32[]{:S(2)}) %all-to-all-start.3) | async-done | bytes 3145760 | tf_op jit(solution)/shard_map/all_to_all | solution.py:298
  120.8 4.3 %all-to-all-start.1 = ((bf16[8,56,2048]{2,1,0:T(8,128)(2,1)}), bf16[8,56,2048]{2,1,0:T(8,128)(2,1)}, u32[]{:S(2)}, u32[]{:S(2)}) async-start(bf16[8,56,2048]{2,1,0:T(8,128)(2,1)} %copy-done.3), calls=%async_computation.1 | async-start | bytes 3670016 | tf_op jit(solution)/shard_map/all_to_all | solution.py:298
  128.8 5.1 %shard_map.132 = (bf16[768,1024]{1,0:T(8,128)(2,1)S(1)}, bf16[768,1024]{1,0:T(8,128)(2,1)S(1)}, bf16[768,512]{1,0:T(8,128)(2,1)S(1)}) custom-call(bf16[768,2048]{1,0:T(8,128)(2,1)S(1)} %bitcast.51, bf16[1024,512]{1,0:T(8,128)(2,1)S(1)} %bitcast.55, bf16[1024,512]{1,0:T(8,128)(2,1)S(1)} %bitcast.57, bf16[512,1024]{1,0:T(8,128)(2,1)S(1)} %bitcast.59), custom_call_target="tpu_custom_call" | custom-call | flops 4026531840 | bytes 10223616 | tf_op jit(solution)/shard_map/pallas_call | solution.py:195
  137.2 12.7 %all-to-all-done.1 = bf16[8,56,2048]{2,1,0:T(8,128)(2,1)} async-done(((bf16[8,56,2048]{2,1,0:T(8,128)(2,1)}), bf16[8,56,2048]{2,1,0:T(8,128)(2,1)}, u32[]{:S(2)}, u32[]{:S(2)}) %all-to-all-start.1) | async-done | bytes 1835040 | tf_op jit(solution)/shard_map/all_to_all | solution.py:298
  149.9 4.5 %all-to-all-start.4 = ((bf16[8,96,1024]{2,1,0:T(8,128)(2,1)}), bf16[8,96,1024]{2,1,0:T(8,128)(2,1)}, u32[]{:S(2)}, u32[]{:S(2)}) async-start(bf16[8,96,1024]{2,1,0:T(8,128)(2,1)} %bitcast.54), calls=%async_computation.4 | async-start | bytes 3145728 | tf_op jit(solution)/shard_map/all_to_all | solution.py:304
  158.2 5.6 %shard_map.130 = (bf16[448,1024]{1,0:T(8,128)(2,1)}, bf16[448,1024]{1,0:T(8,128)(2,1)S(1)}, bf16[448,512]{1,0:T(8,128)(2,1)S(1)}) custom-call(bf16[448,2048]{1,0:T(8,128)(2,1)} %bitcast.5.got_ref.refs_0_.refs_1_, bf16[1024,512]{1,0:T(8,128)(2,1)S(1)} %bitcast.56, bf16[1024,512]{1,0:T(8,128)(2,1)S(1)} %bitcast.58, bf16[512,1024]{1,0:T(8,128)(2,1)S(1)} %bitcast.60), custom_call_target="tpu_custom_call" | custom-call | flops 2348810240 | bytes 7274496 | tf_op jit(solution)/shard_map/pallas_call | solution.py:195
  163.8 7.4 %shard_map.133 = (bf16[2,1536,256]{2,1,0:T(8,128)(2,1)S(1)}, f32[2,1536,256]{2,1,0:T(8,128)S(1)}) custom-call(s32[1]{0:T(128)} %bitcast.13.core_ref, bf16[448,2048]{1,0:T(8,128)(2,1)} %bitcast.5.got_ref.refs_0_.refs_1_, bf16[448,2048]{1,0:T(8,128)(2,1)} %bitcast.5.got_ref.refs_0_.refs_1_, bf16[448,1024]{1,0:T(8,128)(2,1)S(1)} %get-tuple-element.31.refs_2_, ...), custom_call_target="tpu_custom_call" | custom-call | flops 3825205248 | bytes 16777216 | tf_op jit(solution)/shard_map/pallas_call | solution.py:260
  175.5 2.7 %fusion.30 = (bf16[640,1024]{1,0:T(8,128)(2,1)S(1)}, f32[640,1024]{1,0:T(8,128)S(1)}) fusion(bf16[8,96,1024]{2,1,0:T(8,128)(2,1)} %all-to-all-done.4, f32[8,640]{1,0:T(8,128)S(1)} %get-tuple-element.28, f32[96]{0:T(128)S(1)} %iota_convert_fusion), kind=kOutput, calls=%fused_computation.67 | convolution fusion | flops 1007779840 | bytes 5525888 | tf_op jit(solution)/shard_map/dot_general | solution.py:24
  180.4 5.1 %all-to-all-start.2 = ((bf16[8,56,1024]{2,1,0:T(8,128)(2,1)}), bf16[8,56,1024]{2,1,0:T(8,128)(2,1)}, u32[]{:S(2)}, u32[]{:S(2)}) async-start(bf16[8,56,1024]{2,1,0:T(8,128)(2,1)} %bitcast.9), calls=%async_computation.2 | async-start | bytes 1835008 | tf_op jit(solution)/shard_map/all_to_all | solution.py:304
  188.3 2.4 collective-permute-start.13
  194.3 5.0 %collective-permute-done.9 = bf16[128,1024]{1,0:T(8,128)(2,1)} collective-permute-done((bf16[128,1024]{1,0:T(8,128)(2,1)}, bf16[128,1024]{1,0:T(8,128)(2,1)}, u32[]{:S(2)}, u32[]{:S(2)}) %collective-permute-start.9) | collective-permute-done | bytes 262176 | tf_op jit(solution)/shard_map/ppermute | solution.py:32
  201.4 2.7 collective-permute-start.14
  206.1 5.3 %collective-permute-start.23 = (bf16[2,1536,256]{2,1,0:T(8,128)(2,1)S(1)}, bf16[2,1536,256]{2,1,0:T(8,128)(2,1)S(1)}, u32[]{:S(2)}, u32[]{:S(2)}) collective-permute-start(bf16[2,1536,256]{2,1,0:T(8,128)(2,1)S(1)} %copy-done.7), channel_id=1, source_target_pairs={{0,64},{64,0},{1,65},{65,1},{2,66},{66,2},{3,67},{67,3},{4,68},{68... | collective-permute-start | bytes 4718600 | tf_op jit(solution)/shard_map/ppermute | solution.py:36
  211.6 2.7 collective-permute-start.15
  218.6 3.7 %collective-permute-start.16 = (bf16[128,1024]{1,0:T(8,128)(2,1)S(1)}, bf16[128,1024]{1,0:T(8,128)(2,1)S(1)}, u32[]{:S(2)}, u32[]{:S(2)}) collective-permute-start(bf16[128,1024]{1,0:T(8,128)(2,1)S(1)} %get-tuple-element.42), channel_id=1, source_target_pairs={{0,64},{64,0},{1,65},{65,1},{2,66},{66,2},{3,67},{67,3},{4,68},{68... | collective-permute-start | bytes 786440 | tf_op jit(solution)/shard_map/ppermute | solution.py:36
  222.8 2.6 collective-permute-start.19
  228.9 3.2 %collective-permute-done.17 = bf16[128,1024]{1,0:T(8,128)(2,1)S(1)} collective-permute-done((bf16[128,1024]{1,0:T(8,128)(2,1)S(1)}, bf16[128,1024]{1,0:T(8,128)(2,1)S(1)}, u32[]{:S(2)}, u32[]{:S(2)}) %collective-permute-start.17) | collective-permute-done | bytes 262176 | tf_op jit(solution)/shard_map/ppermute | solution.py:341
  232.7 4.9 %collective-permute-start.20 = (bf16[128,1024]{1,0:T(8,128)(2,1)S(1)}, bf16[128,1024]{1,0:T(8,128)(2,1)S(1)}, u32[]{:S(2)}, u32[]{:S(2)}) collective-permute-start(bf16[128,1024]{1,0:T(8,128)(2,1)S(1)} %collective-permute-done.19), channel_id=1, source_target_pairs={{0,64},{64,0},{1,65},{65,1},{2,66},{66,2},{3,67},{67,3},{4,68},{68... | collective-permute-start | bytes 786440 | tf_op jit(solution)/shard_map/ppermute | solution.py:36
  241.9 2.6 fusion.5
  244.5 7.5 %all-to-all-start.5 = ((bf16[32,8,1024]{2,1,0:T(8,128)(2,1)}), bf16[32,8,1024]{2,1,0:T(8,128)(2,1)}, u32[]{:S(2)}, u32[]{:S(2)}) async-start(bf16[32,8,1024]{2,1,0:T(8,128)(2,1)} %fusion.5), calls=%async_computation.5 | async-start | bytes 1048576 | tf_op jit(solution)/shard_map/all_to_all | solution.py:351
  252.0 8.4 %collective-permute-done.24 = bf16[1536,256]{1,0:T(8,128)(2,1)} collective-permute-done((bf16[1536,256]{1,0:T(8,128)(2,1)}, bf16[1536,256]{1,0:T(8,128)(2,1)}, u32[]{:S(2)}, u32[]{:S(2)}) %collective-permute-start.24) | collective-permute-done | bytes 786464 | tf_op jit(solution)/shard_map/ppermute | solution.py:36
  (132 shorter events, 64.6 us)
Async XLA Ops:
  5.5 22.5 %collective-permute-start = (bf16[128,2176]{1,0:T(8,128)(2,1)}, bf16[128,2176]{1,0:T(8,128)(2,1)S(1)}, u32[]{:S(2)}, u32[]{:S(2)}) collective-permute-start(bf16[128,2176]{1,0:T(8,128)(2,1)} %shard_map.128.refs_0_), channel_id=1, source_target_pairs={{0,1},{1,2},{2,3},{3,4},{4,5},{5,6},{6,7},{7,0},{8,9},{9,10},{10,1... | collective-permute-start | bytes 1671176 | tf_op jit(solution)/shard_map/ppermute | solution.py:32
  8.0 20.0 %collective-permute-start.1 = (bf16[128,2176]{1,0:T(8,128)(2,1)}, bf16[128,2176]{1,0:T(8,128)(2,1)S(1)}, u32[]{:S(2)}, u32[]{:S(2)}) collective-permute-start(bf16[128,2176]{1,0:T(8,128)(2,1)} %shard_map.128.refs_0_), channel_id=1, source_target_pairs={{0,7},{1,0},{2,1},{3,2},{4,3},{5,4},{6,5},{7,6},{8,15},{9,8},{10,9... | collective-permute-start | bytes 1671176 | tf_op jit(solution)/shard_map/ppermute | solution.py:32
  28.0 14.3 %collective-permute-start.3 = (bf16[128,2176]{1,0:T(8,128)(2,1)S(1)}, bf16[128,2176]{1,0:T(8,128)(2,1)S(1)}, u32[]{:S(2)}, u32[]{:S(2)}) collective-permute-start(bf16[128,2176]{1,0:T(8,128)(2,1)S(1)} %collective-permute-done.1.refs_2_), channel_id=1, source_target_pairs={{0,7},{1,0},{2,1},{3,2},{4,3},{5,4},{6,5},{7,6},{8,15},{9,8},{10,9... | collective-permute-start | bytes 1671176 | tf_op jit(solution)/shard_map/ppermute | solution.py:32
  30.5 15.1 %collective-permute-start.2 = (bf16[128,2176]{1,0:T(8,128)(2,1)S(1)}, bf16[128,2176]{1,0:T(8,128)(2,1)S(1)}, u32[]{:S(2)}, u32[]{:S(2)}) collective-permute-start(bf16[128,2176]{1,0:T(8,128)(2,1)S(1)} %collective-permute-done.refs_1_), channel_id=1, source_target_pairs={{0,1},{1,2},{2,3},{3,4},{4,5},{5,6},{6,7},{7,0},{8,9},{9,10},{10,1... | collective-permute-start | bytes 1671176 | tf_op jit(solution)/shard_map/ppermute | solution.py:32
  42.2 14.1 %collective-permute-start.5 = (bf16[128,2176]{1,0:T(8,128)(2,1)S(1)}, bf16[128,2176]{1,0:T(8,128)(2,1)S(1)}, u32[]{:S(2)}, u32[]{:S(2)}) collective-permute-start(bf16[128,2176]{1,0:T(8,128)(2,1)S(1)} %collective-permute-done.3.refs_1_), channel_id=1, source_target_pairs={{0,7},{1,0},{2,1},{3,2},{4,3},{5,4},{6,5},{7,6},{8,15},{9,8},{10,9... | collective-permute-start | bytes 1671176 | tf_op jit(solution)/shard_map/ppermute | solution.py:32
  45.7 14.2 %collective-permute-start.4 = (bf16[128,2176]{1,0:T(8,128)(2,1)S(1)}, bf16[128,2176]{1,0:T(8,128)(2,1)S(1)}, u32[]{:S(2)}, u32[]{:S(2)}) collective-permute-start(bf16[128,2176]{1,0:T(8,128)(2,1)S(1)} %collective-permute-done.2.refs_0_), channel_id=1, source_target_pairs={{0,1},{1,2},{2,3},{3,4},{4,5},{5,6},{6,7},{7,0},{8,9},{9,10},{10,1... | collective-permute-start | bytes 1671176 | tf_op jit(solution)/shard_map/ppermute | solution.py:32
  56.4 10.6 %collective-permute-start.7 = (bf16[128,1152]{1,0:T(8,128)(2,1)S(1)}, bf16[128,1152]{1,0:T(8,128)(2,1)S(1)}, u32[]{:S(2)}, u32[]{:S(2)}) collective-permute-start(bf16[128,1152]{1,0:T(8,128)(2,1)S(1)} %slice.79), channel_id=1, source_target_pairs={{0,7},{1,0},{2,1},{3,2},{4,3},{5,4},{6,5},{7,6},{8,15},{9,8},{10,9... | collective-permute-start | bytes 884744 | tf_op jit(solution)/shard_map/ppermute | solution.py:32
  59.9 7.1 %collective-permute-start.6 = (bf16[128,1024]{1,0:T(8,128)(2,1)S(1)}, bf16[128,1024]{1,0:T(8,128)(2,1)S(1)}, u32[]{:S(2)}, u32[]{:S(2)}) collective-permute-start(bf16[128,1024]{1,0:T(8,128)(2,1)S(1)} %slice.78), channel_id=1, source_target_pairs={{0,1},{1,2},{2,3},{3,4},{4,5},{5,6},{6,7},{7,0},{8,9},{9,10},{10,1... | collective-permute-start | bytes 786440 | tf_op jit(solution)/shard_map/ppermute | solution.py:32
  73.8 47.0 %all-to-all-start.3 = ((bf16[8,96,2048]{2,1,0:T(8,128)(2,1)}), bf16[8,96,2048]{2,1,0:T(8,128)(2,1)S(1)}, u32[]{:S(2)}, u32[]{:S(2)}) async-start(bf16[8,96,2048]{2,1,0:T(8,128)(2,1)} %copy-done), calls=%async_computation.3 | async-start | bytes 6291456 | tf_op jit(solution)/shard_map/all_to_all | solution.py:298
  120.8 29.1 %all-to-all-start.1 = ((bf16[8,56,2048]{2,1,0:T(8,128)(2,1)}), bf16[8,56,2048]{2,1,0:T(8,128)(2,1)}, u32[]{:S(2)}, u32[]{:S(2)}) async-start(bf16[8,56,2048]{2,1,0:T(8,128)(2,1)} %copy-done.3), calls=%async_computation.1 | async-start | bytes 3670016 | tf_op jit(solution)/shard_map/all_to_all | solution.py:298
  149.9 25.6 %all-to-all-start.4 = ((bf16[8,96,1024]{2,1,0:T(8,128)(2,1)}), bf16[8,96,1024]{2,1,0:T(8,128)(2,1)}, u32[]{:S(2)}, u32[]{:S(2)}) async-start(bf16[8,96,1024]{2,1,0:T(8,128)(2,1)} %bitcast.54), calls=%async_computation.4 | async-start | bytes 3145728 | tf_op jit(solution)/shard_map/all_to_all | solution.py:304
  179.0 6.6 %collective-permute-start.12 = (bf16[128,512]{1,0:T(8,128)(2,1)}, bf16[128,512]{1,0:T(8,128)(2,1)}, u32[]{:S(2)}, u32[]{:S(2)}) collective-permute-start(bf16[128,512]{1,0:T(8,128)(2,1)} %get-tuple-element.52), channel_id=1, source_target_pairs={{0,7},{1,0},{2,1},{3,2},{4,3},{5,4},{6,5},{7,6},{8,15},{9,8},{10,9... | collective-permute-start | bytes 393224 | tf_op jit(solution)/shard_map/ppermute | solution.py:32
  180.3 5.3 %collective-permute-start.8 = (bf16[128,512]{1,0:T(8,128)(2,1)}, bf16[128,512]{1,0:T(8,128)(2,1)}, u32[]{:S(2)}, u32[]{:S(2)}) collective-permute-start(bf16[128,512]{1,0:T(8,128)(2,1)} %get-tuple-element.51), channel_id=1, source_target_pairs={{0,1},{1,2},{2,3},{3,4},{4,5},{5,6},{6,7},{7,0},{8,9},{9,10},{10,1... | collective-permute-start | bytes 393224 | tf_op jit(solution)/shard_map/ppermute | solution.py:32
  180.4 23.6 %all-to-all-start.2 = ((bf16[8,56,1024]{2,1,0:T(8,128)(2,1)}), bf16[8,56,1024]{2,1,0:T(8,128)(2,1)}, u32[]{:S(2)}, u32[]{:S(2)}) async-start(bf16[8,56,1024]{2,1,0:T(8,128)(2,1)} %bitcast.9), calls=%async_computation.2 | async-start | bytes 1835008 | tf_op jit(solution)/shard_map/all_to_all | solution.py:304
  188.3 6.1 %collective-permute-start.13 = (bf16[128,1024]{1,0:T(8,128)(2,1)}, bf16[128,1024]{1,0:T(8,128)(2,1)}, u32[]{:S(2)}, u32[]{:S(2)}) collective-permute-start(bf16[128,1024]{1,0:T(8,128)(2,1)} %pad_maximum_fusion.1), channel_id=1, source_target_pairs={{0,7},{1,0},{2,1},{3,2},{4,3},{5,4},{6,5},{7,6},{8,15},{9,8},{10,9... | collective-permute-start | bytes 786440 | tf_op jit(solution)/shard_map/ppermute | solution.py:32
  192.3 7.0 %collective-permute-start.9 = (bf16[128,1024]{1,0:T(8,128)(2,1)}, bf16[128,1024]{1,0:T(8,128)(2,1)}, u32[]{:S(2)}, u32[]{:S(2)}) collective-permute-start(bf16[128,1024]{1,0:T(8,128)(2,1)} %pad_maximum_fusion), channel_id=1, source_target_pairs={{0,1},{1,2},{2,3},{3,4},{4,5},{5,6},{6,7},{7,0},{8,9},{9,10},{10,1... | collective-permute-start | bytes 786440 | tf_op jit(solution)/shard_map/ppermute | solution.py:32
  201.3 10.0 %collective-permute-start.10 = (bf16[128,1024]{1,0:T(8,128)(2,1)}, bf16[128,1024]{1,0:T(8,128)(2,1)S(1)}, u32[]{:S(2)}, u32[]{:S(2)}) collective-permute-start(bf16[128,1024]{1,0:T(8,128)(2,1)} %get-tuple-element.43), channel_id=1, source_target_pairs={{0,1},{1,2},{2,3},{3,4},{4,5},{5,6},{6,7},{7,0},{8,9},{9,10},{10,1... | collective-permute-start | bytes 786440 | tf_op jit(solution)/shard_map/ppermute | solution.py:32
  201.4 10.0 %collective-permute-start.14 = (bf16[128,1024]{1,0:T(8,128)(2,1)}, bf16[128,1024]{1,0:T(8,128)(2,1)S(1)}, u32[]{:S(2)}, u32[]{:S(2)}) collective-permute-start(bf16[128,1024]{1,0:T(8,128)(2,1)} %get-tuple-element.44), channel_id=1, source_target_pairs={{0,7},{1,0},{2,1},{3,2},{4,3},{5,4},{6,5},{7,6},{8,15},{9,8},{10,9... | collective-permute-start | bytes 786440 | tf_op jit(solution)/shard_map/ppermute | solution.py:32
  206.1 33.5 %collective-permute-start.23 = (bf16[2,1536,256]{2,1,0:T(8,128)(2,1)S(1)}, bf16[2,1536,256]{2,1,0:T(8,128)(2,1)S(1)}, u32[]{:S(2)}, u32[]{:S(2)}) collective-permute-start(bf16[2,1536,256]{2,1,0:T(8,128)(2,1)S(1)} %copy-done.7), channel_id=1, source_target_pairs={{0,64},{64,0},{1,65},{65,1},{2,66},{66,2},{3,67},{67,3},{4,68},{68... | collective-permute-start | bytes 4718600 | tf_op jit(solution)/shard_map/ppermute | solution.py:36
  211.5 6.5 %collective-permute-start.11 = (bf16[128,1024]{1,0:T(8,128)(2,1)S(1)}, bf16[128,1024]{1,0:T(8,128)(2,1)S(1)}, u32[]{:S(2)}, u32[]{:S(2)}) collective-permute-start(bf16[128,1024]{1,0:T(8,128)(2,1)S(1)} %get-tuple-element.49), channel_id=1, source_target_pairs={{0,1},{1,2},{2,3},{3,4},{4,5},{5,6},{6,7},{7,0},{8,9},{9,10},{10,1... | collective-permute-start | bytes 786440 | tf_op jit(solution)/shard_map/ppermute | solution.py:32
  211.6 6.4 %collective-permute-start.15 = (bf16[128,1024]{1,0:T(8,128)(2,1)S(1)}, bf16[128,1024]{1,0:T(8,128)(2,1)S(1)}, u32[]{:S(2)}, u32[]{:S(2)}) collective-permute-start(bf16[128,1024]{1,0:T(8,128)(2,1)S(1)} %get-tuple-element.50), channel_id=1, source_target_pairs={{0,7},{1,0},{2,1},{3,2},{4,3},{5,4},{6,5},{7,6},{8,15},{9,8},{10,9... | collective-permute-start | bytes 786440 | tf_op jit(solution)/shard_map/ppermute | solution.py:32
  218.3 21.3 %copy-start.2 = (f32[2,1536,256]{2,1,0:T(8,128)S(1)}, f32[2,1536,256]{2,1,0:T(8,128)}, u32[]{:S(2)}) copy-start(f32[2,1536,256]{2,1,0:T(8,128)} %copy-done.1) | copy-start | bytes 9437188
  218.6 21.0 %copy-start.25 = (bf16[128,1024]{1,0:T(8,128)(2,1)}, bf16[128,1024]{1,0:T(8,128)(2,1)S(1)}, u32[]{:S(2)}) copy-start(bf16[128,1024]{1,0:T(8,128)(2,1)S(1)} %get-tuple-element.42) | copy-start | bytes 786436
  218.6 20.9 %collective-permute-start.16 = (bf16[128,1024]{1,0:T(8,128)(2,1)S(1)}, bf16[128,1024]{1,0:T(8,128)(2,1)S(1)}, u32[]{:S(2)}, u32[]{:S(2)}) collective-permute-start(bf16[128,1024]{1,0:T(8,128)(2,1)S(1)} %get-tuple-element.42), channel_id=1, source_target_pairs={{0,64},{64,0},{1,65},{65,1},{2,66},{66,2},{3,67},{67,3},{4,68},{68... | collective-permute-start | bytes 786440 | tf_op jit(solution)/shard_map/ppermute | solution.py:36
  222.2 9.8 %collective-permute-start.17 = (bf16[128,1024]{1,0:T(8,128)(2,1)S(1)}, bf16[128,1024]{1,0:T(8,128)(2,1)S(1)}, u32[]{:S(2)}, u32[]{:S(2)}) collective-permute-start(bf16[128,1024]{1,0:T(8,128)(2,1)S(1)} %get-tuple-element.42), channel_id=1, source_target_pairs={{0,128},{128,8},{8,136},{136,0},{1,129},{129,9},{9,137},{137,1},{2... | collective-permute-start | bytes 786440 | tf_op jit(solution)/shard_map/ppermute | solution.py:341
  222.8 9.9 %collective-permute-start.19 = (bf16[128,1024]{1,0:T(8,128)(2,1)S(1)}, bf16[128,1024]{1,0:T(8,128)(2,1)S(1)}, u32[]{:S(2)}, u32[]{:S(2)}) collective-permute-start(bf16[128,1024]{1,0:T(8,128)(2,1)S(1)} %get-tuple-element.42), channel_id=1, source_target_pairs={{0,136},{128,0},{8,128},{136,8},{1,137},{129,1},{9,129},{137,9},{2... | collective-permute-start | bytes 786440 | tf_op jit(solution)/shard_map/ppermute | solution.py:341
  225.4 13.2 %collective-permute-start.21 = (bf16[128,1024]{1,0:T(8,128)(2,1)S(1)}, bf16[128,1024]{1,0:T(8,128)(2,1)S(1)}, u32[]{:S(2)}, u32[]{:S(2)}) collective-permute-start(bf16[128,1024]{1,0:T(8,128)(2,1)S(1)} %get-tuple-element.42), channel_id=1, source_target_pairs={{0,8},{128,136},{8,0},{136,128},{1,9},{129,137},{9,1},{137,129},{2... | collective-permute-start | bytes 786440 | tf_op jit(solution)/shard_map/ppermute | solution.py:341
  232.0 9.8 %collective-permute-start.18 = (bf16[128,1024]{1,0:T(8,128)(2,1)S(1)}, bf16[128,1024]{1,0:T(8,128)(2,1)S(1)}, u32[]{:S(2)}, u32[]{:S(2)}) collective-permute-start(bf16[128,1024]{1,0:T(8,128)(2,1)S(1)} %collective-permute-done.17), channel_id=1, source_target_pairs={{0,64},{64,0},{1,65},{65,1},{2,66},{66,2},{3,67},{67,3},{4,68},{68... | collective-permute-start | bytes 786440 | tf_op jit(solution)/shard_map/ppermute | solution.py:36
  232.7 9.1 %collective-permute-start.20 = (bf16[128,1024]{1,0:T(8,128)(2,1)S(1)}, bf16[128,1024]{1,0:T(8,128)(2,1)S(1)}, u32[]{:S(2)}, u32[]{:S(2)}) collective-permute-start(bf16[128,1024]{1,0:T(8,128)(2,1)S(1)} %collective-permute-done.19), channel_id=1, source_target_pairs={{0,64},{64,0},{1,65},{65,1},{2,66},{66,2},{3,67},{67,3},{4,68},{68... | collective-permute-start | bytes 786440 | tf_op jit(solution)/shard_map/ppermute | solution.py:36
  238.6 3.3 %collective-permute-start.22 = (bf16[128,1024]{1,0:T(8,128)(2,1)S(1)}, bf16[128,1024]{1,0:T(8,128)(2,1)S(1)}, u32[]{:S(2)}, u32[]{:S(2)}) collective-permute-start(bf16[128,1024]{1,0:T(8,128)(2,1)S(1)} %collective-permute-done.21), channel_id=1, source_target_pairs={{0,64},{64,0},{1,65},{65,1},{2,66},{66,2},{3,67},{67,3},{4,68},{68... | collective-permute-start | bytes 786440 | tf_op jit(solution)/shard_map/ppermute | solution.py:36
  240.9 19.5 %collective-permute-start.24 = (bf16[1536,256]{1,0:T(8,128)(2,1)}, bf16[1536,256]{1,0:T(8,128)(2,1)}, u32[]{:S(2)}, u32[]{:S(2)}) collective-permute-start(bf16[1536,256]{1,0:T(8,128)(2,1)} %fusion.8), channel_id=1, source_target_pairs={{0,128},{128,0},{1,129},{129,1},{2,130},{130,2},{3,131},{131,3},{4... | collective-permute-start | bytes 2359304 | tf_op jit(solution)/shard_map/ppermute | solution.py:36
  244.5 21.4 %all-to-all-start.5 = ((bf16[32,8,1024]{2,1,0:T(8,128)(2,1)}), bf16[32,8,1024]{2,1,0:T(8,128)(2,1)}, u32[]{:S(2)}, u32[]{:S(2)}) async-start(bf16[32,8,1024]{2,1,0:T(8,128)(2,1)} %fusion.5), calls=%async_computation.5 | async-start | bytes 1048576 | tf_op jit(solution)/shard_map/all_to_all | solution.py:351
  (25 other events, 87.8 us)
where the time goes:
time: 272 us; the launch traced here: 268 us
  waiting for transfers between devices  101 us (37%)
  starting transfers between devices  70.4 us (26%)
  local copies, waits for them, and re-layouts  34.3 us (13%)
  Pallas kernels  28.7 us (11%)
  blocking collectives  14.7 us (5%)
  other arithmetic  10.4 us (4%)
  matrix products  7.26 us (3%)
    all_to_all x2, waiting for transfers between devices, send(): lax.all_to_all(sent, ('x', 'yhi'), split_axis=0, concat_axis=0, tiled=True)  47.7 us
    ppermute x16, waiting for transfers between devices, shift_z(): lax.ppermute(block, 'z', [(i, (i + step) % RING) for i in range(RING)])  36.7 us
    unnamed x70, local copies, waits for them, and re-layouts  29.9 us
    ppermute x16, starting transfers between devices, shift_z(): lax.ppermute(block, 'z', [(i, (i + step) % RING) for i in range(RING)])  24 us
    ppermute x6, starting transfers between devices, swap(): return lax.ppermute(block, axis, [(0, 1), (1, 0)])  16.3 us
    all_to_all x1, blocking collectives, body(): lax.all_to_all(attn, ('ylo', 'core', 'yhi'), split_axis=0, concat_axis=0,...  14.7 us
    pallas_call x2, Pallas kernels, run_expert(): pl.pallas_call(expert_kernel, grid=(steps,), in_specs=[pl.BlockSpec((rows...  10.7 us
    all_to_all x2, starting transfers between devices, answer(): lax.all_to_all(back, ('x', 'yhi'), split_axis=0, concat_axis=0, tiled=True)  9.57 us
  transfers between devices with their start and end apart: 30, of which 15 were waited for; matrix products, arithmetic and copies ran while one was open for 8% of the time, Pallas kernels for 8%

commit v1 on v0

--- a/solution.py
+++ b/solution.py
@@ -60,32 +60,35 @@
     return blocks[0] + got_right + got_left
 
 
-def enter_kernel(resid_ref, grad_ref, gain_ref, ids_ref, vals_ref, out_ref):
+def enter_kernel(resid_ref, grad_ref, gain_ref, ids_ref, vals_ref, in_ref, out_ref):
     tokens, feature = resid_ref.shape
     resid = resid_ref[...].astype(f32)
     inv_rms = lax.rsqrt(jnp.mean(resid * resid, axis=1, keepdims=True) + epsilon)
-    out_ref[:, :feature] = (resid * inv_rms * gain_ref[...]).astype(bf16)
-    out_ref[:, feature : 2 * feature] = grad_ref[...]
+    in_ref[...] = (resid * inv_rms * gain_ref[...]).astype(bf16)
+    out_ref[:, :feature] = grad_ref[...]
     vals = vals_ref[...]
     high = vals.astype(bf16).astype(f32)
     middle = (vals - high).astype(bf16).astype(f32)
     low = vals - high - middle
-    rest = jnp.zeros((tokens, META - 4 * TOP), f32)
-    meta = jnp.concatenate([ids_ref[...].astype(f32), high, middle, low, rest], axis=1)
-    out_ref[:, 2 * feature :] = meta.astype(bf16)
+    rest = jnp.zeros((META - 4 * TOP, tokens), f32)
+    meta = jnp.concatenate([ids_ref[...].astype(f32), high, middle, low, rest], axis=0)
+    out_ref[:, feature:] = meta.T.astype(bf16)
 
 
 def enter(resid, out_grad, gain, expert_ids, gate_vals):
     tokens, feature = resid.shape
     return pl.pallas_call(
         enter_kernel,
-        out_shape=jax.ShapeDtypeStruct((tokens, 2 * feature + META), bf16),
-    )(resid, out_grad, gain.reshape(1, feature), expert_ids, gate_vals)
-
-
-def pick_kernel(layout, z_ref, *refs):
+        out_shape=[
+            jax.ShapeDtypeStruct((tokens, feature), bf16),
+            jax.ShapeDtypeStruct((tokens, feature + META), bf16),
+        ],
+    )(resid, out_grad, gain.reshape(1, feature), expert_ids.T, gate_vals.T)
+
+
+def pick_kernel(layout, first, offset, z_ref, *refs):
     pieces = sum(len(widths) for widths in layout)
-    ins, out_ref, target_ref, held, gates = refs[:pieces], *refs[pieces:]
+    ins, (out_ref, target_ref, held, gates) = refs[:pieces], refs[-4:]
     rows, width = out_ref.shape[1:]
     half = width // 2
     tokens = ins[0].shape[0]
@@ -119,12 +122,12 @@
                 named = jnp.where(same, 1.0, named)
                 gate = jnp.where(same, value[k : k + 1], gate)
             slot = jnp.dot(named.astype(bf16), earlier, preferred_element_type=f32)
-            place = jnp.where(named > 0.5, slot + float(i * CAPACITY), -1.0)
+            place = jnp.where(named > 0.5, slot + float((first + i) * CAPACITY), -1.0)
             target_ref[:, lines] = place
             gates[:, lines] = gate
 
     e = pl.program_id(0)
-    row_ids = lax.broadcasted_iota(jnp.int32, (rows, held.shape[0]), 0).astype(f32)
+    row_ids = (lax.broadcasted_iota(jnp.int32, (rows, held.shape[0]), 0) + offset).astype(f32)
     hit = row_ids == target_ref[pl.ds(e, 1), :]
     gate = jnp.sum(jnp.where(hit, gates[pl.ds(e, 1), :], 0.0), axis=1, keepdims=True)
     onehot = jnp.where(hit, 1.0, 0.0).astype(bf16)
@@ -134,21 +137,22 @@
     out_ref[0, :, half:] = (picked * gate).astype(bf16)
 
 
-def pick_rows(z, blocks, width):
+def pick_rows(z, blocks, width, total, first=0, rows=None, into=None):
     count = len(blocks)
     tokens = blocks[0][0].shape[0]
-    rows = -(-count * CAPACITY // 8) * 8
+    rows = rows or total
+    at = total // rows - 1
     flat = [piece for block in blocks for piece in block]
     layout = tuple(tuple(piece.shape[1] for piece in block) for block in blocks)
     whole = [pl.BlockSpec(piece.shape, lambda e, z: (0, 0)) for piece in flat]
     return pl.pallas_call(
-        functools.partial(pick_kernel, layout),
+        functools.partial(pick_kernel, layout, first, total - rows),
         grid_spec=pltpu.PrefetchScalarGridSpec(
             num_scalar_prefetch=1,
             grid=(PLANE,),
-            in_specs=whole,
+            in_specs=whole + [pl.BlockSpec(memory_space=pl.ANY)] * (into is not None),
             out_specs=[
-                pl.BlockSpec((1, rows, width), lambda e, z: (e, 0, 0)),
+                pl.BlockSpec((1, rows, width), lambda e, z: (e, at, 0)),
                 pl.BlockSpec((PLANE, count * tokens), lambda e, z: (0, 0)),
             ],
             scratch_shapes=[
@@ -157,16 +161,17 @@
             ],
         ),
         out_shape=[
-            jax.ShapeDtypeStruct((PLANE, rows, width), bf16),
+            jax.ShapeDtypeStruct((PLANE, total, width), bf16),
             jax.ShapeDtypeStruct((PLANE, count * tokens), f32),
         ],
-        compiler_params=pltpu.CompilerParams(vmem_limit_bytes=24 << 20),
+        input_output_aliases={} if into is None else {1 + len(flat): 0},
+        compiler_params=pltpu.CompilerParams(vmem_limit_bytes=56 << 20),
         cost_estimate=pl.CostEstimate(
             flops=2 * PLANE * rows * count * tokens * width,
             bytes_accessed=2 * width * (count * tokens + PLANE * rows),
             transcendentals=0,
         ),
-    )(z.reshape(1), *flat)
+    )(z.reshape(1), *flat, *([] if into is None else [into]))
 
 
 def expert_kernel(got_ref, w_gate_ref, w_up_ref, w_down_ref, back_ref, slopes_ref, hidden_ref):
@@ -211,7 +216,7 @@
             jax.ShapeDtypeStruct((total, 2 * inner), bf16),
             jax.ShapeDtypeStruct((total, inner), bf16),
         ],
-        compiler_params=pltpu.CompilerParams(vmem_limit_bytes=32 << 20),
+        compiler_params=pltpu.CompilerParams(vmem_limit_bytes=56 << 20),
         cost_estimate=pl.CostEstimate(
             flops=10 * total * feature * inner,
             bytes_accessed=2 * total * (width + feature + 3 * inner) + 6 * feature * inner,
@@ -269,7 +274,7 @@
             ],
         ),
         out_shape=[jax.ShapeDtypeStruct(shape, bf16), jax.ShapeDtypeStruct(shape, f32)],
-        compiler_params=pltpu.CompilerParams(vmem_limit_bytes=40 << 20),
+        compiler_params=pltpu.CompilerParams(vmem_limit_bytes=56 << 20),
         cost_estimate=pl.CostEstimate(flops=flops, bytes_accessed=16 << 20, transcendentals=0),
     )(core.reshape(1), *arrays)
 
@@ -282,33 +287,36 @@
     yhi = lax.axis_index("yhi")
     w_gate, w_up, w_down = w_gate[0], w_up[0], w_down[0]
 
-    mine = enter(resid, out_grad, gain, expert_ids, gate_vals)
-    right, left = shift_z(mine, 1), shift_z(mine, -1)
+    own = enter(resid, out_grad, gain, expert_ids, gate_vals)
+    right, left = [shift_z(a, 1) for a in own], [shift_z(a, -1) for a in own]
+    gathered = {0: own, -1: right, 1: left}
+    sent_near, target_near = pick_rows(z, [gathered[d] for d in NEAR], 2 * feature, 56)
     attn = attn_out.reshape(tokens, 2, 2, 4, 2, 64).transpose(1, 2, 4, 0, 3, 5).reshape(8, tokens, 256)
     attn = lax.all_to_all(attn, ("ylo", "core", "yhi"), split_axis=0, concat_axis=0, tiled=True)
-    right, left, attn = lax.optimization_barrier((right, left, attn))
-    gathered = {0: [mine], -1: [right], 1: [left]}
-    for d in (2, 3):
-        right, left = shift_z(right, 1), shift_z(left, -1)
-        gathered[-d], gathered[d] = [right], [left]
-    gathered[4] = [shift_z(right[:, :feature], 1), shift_z(left[:, feature:], -1)]
-
-    def send(deltas):
-        sent, target = pick_rows(z, [gathered[d] for d in deltas], 2 * feature)
-        got = lax.all_to_all(sent, ("x", "yhi"), split_axis=0, concat_axis=0, tiled=True)
-        return got.reshape(-1, 2 * feature), target
-
-    def answer(got, steps):
-        back, slopes, hidden = run_expert(got, w_gate, w_up, w_down, steps)
-        back = back.reshape(PLANE, -1, feature)
-        returned = lax.all_to_all(back, ("x", "yhi"), split_axis=0, concat_axis=0, tiled=True)
-        return returned, (got, slopes, hidden)
-
-    got_near, target_near = send(NEAR)
-    got_far, target_far = send(FAR)
-    returned_near, saved_near = answer(got_near, 2)
-    returned_far, saved_far = answer(got_far, 3)
-    other, own = weight_terms(core, saved_near, saved_far)
+    right, left = [shift_z(a, 1) for a in right], [shift_z(a, -1) for a in left]
+    sent_near, attn, right, left = lax.optimization_barrier((sent_near, attn, right, left))
+    gathered[-2], gathered[2] = right, left
+    right, left = [shift_z(a, 1) for a in right], [shift_z(a, -1) for a in left]
+    gathered[-3], gathered[3] = right, left
+    sent_far, target_far = pick_rows(z, [gathered[d] for d in FAR[:-1]], 2 * feature, 96)
+    sent_far, *last = lax.optimization_barrier((sent_far, shift_z(right[0], 1), shift_z(left[1], -1)))
+    last = [gathered[3], last]
+    sent_far, target_last = pick_rows(z, last, 2 * feature, 96, len(FAR) - 2, 32, sent_far)
+    target_far = jnp.concatenate([target_far, target_last[:, tokens:]], axis=1)
+
+    def over_plane(rows):
+        return lax.all_to_all(rows, ("x", "yhi"), split_axis=0, concat_axis=0, tiled=True)
+
+    got_near = over_plane(sent_near).reshape(-1, 2 * feature)
+    got_near, sent_far = lax.optimization_barrier((got_near, sent_far))
+    got_far = over_plane(sent_far).reshape(-1, 2 * feature)
+    back_near, *saved_near = run_expert(got_near, w_gate, w_up, w_down, 2)
+    back_near, got_far = lax.optimization_barrier((back_near, got_far))
+    returned_near = over_plane(back_near.reshape(PLANE, -1, feature))
+    back_far, *saved_far = run_expert(got_far, w_gate, w_up, w_down, 3)
+    returned_near, back_far = lax.optimization_barrier((returned_near, back_far))
+    returned_far = over_plane(back_far.reshape(PLANE, -1, feature))
+    other, own = weight_terms(core, (got_near, *saved_near), (got_far, *saved_far))
     returned_far, other, own = lax.optimization_barrier((returned_far, other, own))
 
     total = own + swap(other, "core").astype(f32)

time: 272 us -> 245 us (0.901); the launches traced: 268 us -> 243 us
  local copies, waits for them, and re-layouts: 34.3 us -> 8.94 us
  starting transfers between devices: 70.4 us -> 88 us
  Pallas kernels: 28.7 us -> 45.8 us
  waiting for transfers between devices: 101 us -> 86.3 us
  blocking collectives: 14.7 us -> 0 us
  other arithmetic: 10.4 us -> 6.61 us
    unnamed x70 -> x68, local copies, waits for them, and re-layouts: 29.9 us -> 5.13 us
    all_to_all x1 -> x0, blocking collectives: 14.7 us -> none  [body(): lax.all_to_all(attn, ('ylo', 'core', 'yhi'), split_axis=0, concat_axis=0,...]
    all_to_all x4 -> x5, starting transfers between devices: 17.9 us -> 29.8 us  [the longest x4 23.9 us: over_plane(): lax.all_to_all(rows, ('x', 'yhi'), split_axis=0, concat_axis=0, tiled=True)]
    ppermute x16 -> x22, waiting for transfers between devices: 36.7 us -> 25.7 us  [shift_z(): lax.ppermute(block, 'z', [(i, (i + step) % RING) for i in range(RING)])]
    pallas_call x3 -> x4, Pallas kernels: 10.7 us -> 21.3 us  [the longest x3 19.3 us: pick_rows(): pl.pallas_call(functools.partial(pick_kernel, layout, first, total - rows...]
    ppermute x16 -> x22, starting transfers between devices: 24 us -> 31.9 us  [shift_z(): lax.ppermute(block, 'z', [(i, (i + step) % RING) for i in range(RING)])]
    ppermute x6, waiting for transfers between devices: 8.45 us -> 13.1 us  [swap(): return lax.ppermute(block, axis, [(0, 1), (1, 0)])]
    ppermute x3, waiting for transfers between devices: 4.19 us -> 0.03 us  [body(): lax.ppermute(d_resid, ('ylo', 'yhi'), y_peer(step))]
  transfers between devices with their start and end apart: 30 -> 37, of which waited for: 15 -> 13; matrix products, arithmetic and copies ran while one was open for 8% -> 5% of each run, Pallas kernels for 8% -> 18%
where the time goes in v1:
time: 245 us; the launch traced here: 243 us
  starting transfers between devices  88 us (36%)
  waiting for transfers between devices  86.3 us (35%)
  Pallas kernels  45.8 us (19%)
  local copies, waits for them, and re-layouts  8.94 us (4%)
  other arithmetic  6.61 us (3%)
  matrix products  6.37 us (3%)
    all_to_all x4, waiting for transfers between devices, over_plane(): lax.all_to_all(rows, ('x', 'yhi'), split_axis=0, concat_axis=0, tiled=True)  47.5 us
    ppermute x22, starting transfers between devices, shift_z(): lax.ppermute(block, 'z', [(i, (i + step) % RING) for i in range(RING)])  31.9 us
    ppermute x22, waiting for transfers between devices, shift_z(): lax.ppermute(block, 'z', [(i, (i + step) % RING) for i in range(RING)])  25.7 us
    all_to_all x4, starting transfers between devices, over_plane(): lax.all_to_all(rows, ('x', 'yhi'), split_axis=0, concat_axis=0, tiled=True)  23.9 us
    pallas_call x3, Pallas kernels, pick_rows(): pl.pallas_call(functools.partial(pick_kernel, layout, first, total - rows...  19.3 us
    ppermute x6, starting transfers between devices, swap(): return lax.ppermute(block, axis, [(0, 1), (1, 0)])  18.8 us
    pallas_call x2, Pallas kernels, run_expert(): pl.pallas_call(expert_kernel, grid=(steps,), in_specs=[pl.BlockSpec((rows...  14.5 us
    ppermute x6, waiting for transfers between devices, swap(): return lax.ppermute(block, axis, [(0, 1), (1, 0)])  13.1 us
  transfers between devices with their start and end apart: 37, of which 13 were waited for; matrix products, arithmetic and copies ran while one was open for 5% of the time, Pallas kernels for 18%

profile of v1, /device:TPU:1, one launch (start us, length us, event | category | flops | bytes accessed | tf_op | source)
XLA Modules:
  0.0 243.5 jit_solution(7474963894043143916)
XLA Ops:
  2.6 6.4 %collective-permute-start.3 = (bf16[128,1152]{1,0:T(8,128)(2,1)}, bf16[128,1152]{1,0:T(8,128)(2,1)S(1)}, u32[]{:S(2)}, u32[]{:S(2)}) collective-permute-start(bf16[128,1152]{1,0:T(8,128)(2,1)} %get-tuple-element.40.refs_1_), channel_id=1, source_target_pairs={{0,7},{1,0},{2,1},{3,2},{4,3},{5,4},{6,5},{7,6},{8,15},{9,8},{10,9... | collective-permute-start | bytes 884744 | tf_op jit(solution)/shard_map/ppermute | solution.py:32
  9.0 2.7 %collective-permute-start.2 = (bf16[128,1024]{1,0:T(8,128)(2,1)}, bf16[128,1024]{1,0:T(8,128)(2,1)S(1)}, u32[]{:S(2)}, u32[]{:S(2)}) collective-permute-start(bf16[128,1024]{1,0:T(8,128)(2,1)} %get-tuple-element.39.refs_0_), channel_id=1, source_target_pairs={{0,7},{1,0},{2,1},{3,2},{4,3},{5,4},{6,5},{7,6},{8,15},{9,8},{10,9... | collective-permute-start | bytes 786440 | tf_op jit(solution)/shard_map/ppermute | solution.py:32
  13.9 6.0 %all-to-all-start = ((bf16[8,128,256]{1,2,0:T(8,128)(2,1)}), bf16[8,128,256]{1,2,0:T(8,128)(2,1)S(1)}, u32[]{:S(2)}, u32[]{:S(2)}) async-start(bf16[8,128,256]{1,2,0:T(8,128)(2,1)} %bitcast.6), calls=%async_computation | async-start | bytes 1048576 | tf_op jit(solution)/shard_map/all_to_all | solution.py:295
  19.9 3.0 %collective-permute-start.7 = (bf16[128,1152]{1,0:T(8,128)(2,1)S(1)}, bf16[128,1152]{1,0:T(8,128)(2,1)S(1)}, u32[]{:S(2)}, u32[]{:S(2)}) collective-permute-start(bf16[128,1152]{1,0:T(8,128)(2,1)S(1)} %collective-permute-done.3.refs_5_), channel_id=1, source_target_pairs={{0,7},{1,0},{2,1},{3,2},{4,3},{5,4},{6,5},{7,6},{8,15},{9,8},{10,9... | collective-permute-start | bytes 884744 | tf_op jit(solution)/shard_map/ppermute | solution.py:32
  22.9 2.7 %collective-permute-start.6 = (bf16[128,1024]{1,0:T(8,128)(2,1)S(1)}, bf16[128,1024]{1,0:T(8,128)(2,1)S(1)}, u32[]{:S(2)}, u32[]{:S(2)}) collective-permute-start(bf16[128,1024]{1,0:T(8,128)(2,1)S(1)} %collective-permute-done.2.refs_4_), channel_id=1, source_target_pairs={{0,7},{1,0},{2,1},{3,2},{4,3},{5,4},{6,5},{7,6},{8,15},{9,8},{10,9... | collective-permute-start | bytes 786440 | tf_op jit(solution)/shard_map/ppermute | solution.py:32
  26.3 6.5 %shard_map.129 = (bf16[8,56,2048]{2,1,0:T(8,128)(2,1)}, f32[8,384]{1,0:T(8,128)}) custom-call(s32[1]{0:T(128)} %bitcast.z_ref, bf16[128,1024]{1,0:T(8,128)(2,1)} %get-tuple-element.39.refs_0_, bf16[128,1152]{1,0:T(8,128)(2,1)} %get-tuple-element.40.refs_1_, bf16[128,1024]{1,0:T(8,128)(2,1)} %copy-done.24, bf16[128,1152]{1,0:T(8,128)(2,1)} %copy-done.19, ...), custom_call_target="tpu_custom_call" | custom-call | flops 704643072 | bytes 3407872 | tf_op jit(solution)/shard_map/pallas_call | solution.py:148
  34.9 3.1 %collective-permute-done.4.refs_0_ = bf16[128,1024]{1,0:T(8,128)(2,1)S(1)} collective-permute-done((bf16[128,1024]{1,0:T(8,128)(2,1)S(1)}, bf16[128,1024]{1,0:T(8,128)(2,1)S(1)}, u32[]{:S(2)}, u32[]{:S(2)}) %collective-permute-start.4) | collective-permute-done | bytes 262176 | tf_op jit(solution)/shard_map/ppermute | solution.py:32
  38.1 6.2 %all-to-all-start.1 = ((bf16[8,56,2048]{2,1,0:T(8,128)(2,1)}), bf16[8,56,2048]{2,1,0:T(8,128)(2,1)S(1)}, u32[]{:S(2)}, u32[]{:S(2)}) async-start(bf16[8,56,2048]{2,1,0:T(8,128)(2,1)} %get-tuple-element.43), calls=%async_computation.1 | async-start | bytes 3670016 | tf_op jit(solution)/shard_map/all_to_all | solution.py:308
  52.9 3.7 %collective-permute-done.8.refs_6_.refs_0_ = bf16[128,1024]{1,0:T(8,128)(2,1)S(1)} collective-permute-done((bf16[128,1024]{1,0:T(8,128)(2,1)S(1)}, bf16[128,1024]{1,0:T(8,128)(2,1)S(1)}, u32[]{:S(2)}, u32[]{:S(2)}) %collective-permute-start.8) | collective-permute-done | bytes 262176 | tf_op jit(solution)/shard_map/ppermute | solution.py:32
  59.0 7.3 %shard_map.130 = (bf16[8,96,2048]{2,1,0:T(8,128)(2,1)}, f32[8,512]{1,0:T(8,128)}) custom-call(s32[1]{0:T(128)} %bitcast.z_ref, bf16[128,1024]{1,0:T(8,128)(2,1)} %copy-done.22, bf16[128,1152]{1,0:T(8,128)(2,1)} %copy-done.17, bf16[128,1024]{1,0:T(8,128)(2,1)} %copy-done.21, bf16[128,1152]{1,0:T(8,128)(2,1)} %copy-done.16, bf16[128,1024]{1,0:T(8,128)(2,1)} %copy-done.25, ...), custom_call_target="tpu_custom_call" | custom-call | flops 1610612736 | bytes 5242880 | tf_op jit(solution)/shard_map/pallas_call | solution.py:148
  67.1 5.5 %shard_map.131 = (bf16[8,96,2048]{2,1,0:T(8,128)(2,1)}, f32[8,256]{1,0:T(8,128)}) custom-call(s32[1]{0:T(128)} %bitcast.z_ref, bf16[128,1024]{1,0:T(8,128)(2,1)} %copy-done.9, bf16[128,1152]{1,0:T(8,128)(2,1)} %copy-done.7, bf16[128,1024]{1,0:T(8,128)(2,1)} %copy-done.10, bf16[128,1152]{1,0:T(8,128)(2,1)} %copy-done.8, ...), custom_call_target="tpu_custom_call", output_to_operand_aliasing={{0}: (5, {})} | custom-call | flops 268435456 | bytes 2097152 | tf_op jit(solution)/shard_map/pallas_call | solution.py:148
  73.9 6.4 %all-to-all-start.2 = ((bf16[8,96,2048]{2,1,0:T(8,128)(2,1)}), bf16[8,96,2048]{2,1,0:T(8,128)(2,1)S(1)}, u32[]{:S(2)}, u32[]{:S(2)}) async-start(bf16[8,96,2048]{2,1,0:T(8,128)(2,1)} %get-tuple-element.55), calls=%async_computation.2 | async-start | bytes 6291456 | tf_op jit(solution)/shard_map/all_to_all | solution.py:308
  80.3 6.4 %shard_map.132 = (bf16[448,1024]{1,0:T(8,128)(2,1)}, bf16[448,1024]{1,0:T(8,128)(2,1)}, bf16[448,512]{1,0:T(8,128)(2,1)}) custom-call(bf16[448,2048]{1,0:T(8,128)(2,1)} %bitcast.65, bf16[1024,512]{1,0:T(8,128)(2,1)} %bitcast.73, bf16[1024,512]{1,0:T(8,128)(2,1)} %bitcast.75, bf16[512,1024]{1,0:T(8,128)(2,1)} %bitcast.77), custom_call_target="tpu_custom_call" | custom-call | flops 2348810240 | bytes 7274496 | tf_op jit(solution)/shard_map/pallas_call | solution.py:200
  86.7 34.0 %all-to-all-done.2 = bf16[8,96,2048]{2,1,0:T(8,128)(2,1)S(1)} async-done(((bf16[8,96,2048]{2,1,0:T(8,128)(2,1)}), bf16[8,96,2048]{2,1,0:T(8,128)(2,1)S(1)}, u32[]{:S(2)}, u32[]{:S(2)}) %all-to-all-start.2) | async-done | bytes 3145760 | tf_op jit(solution)/shard_map/all_to_all | solution.py:308
  120.6 4.2 %all-to-all-start.3 = ((bf16[8,56,1024]{2,1,0:T(8,128)(2,1)}), bf16[8,56,1024]{2,1,0:T(8,128)(2,1)}, u32[]{:S(2)}, u32[]{:S(2)}) async-start(bf16[8,56,1024]{2,1,0:T(8,128)(2,1)} %bitcast.69), calls=%async_computation.3 | async-start | bytes 1835008 | tf_op jit(solution)/shard_map/all_to_all | solution.py:308
  124.9 8.1 %shard_map.133 = (bf16[768,1024]{1,0:T(8,128)(2,1)}, bf16[768,1024]{1,0:T(8,128)(2,1)}, bf16[768,512]{1,0:T(8,128)(2,1)}) custom-call(bf16[768,2048]{1,0:T(8,128)(2,1)} %bitcast.53, bf16[1024,512]{1,0:T(8,128)(2,1)} %bitcast.74, bf16[1024,512]{1,0:T(8,128)(2,1)} %bitcast.76, bf16[512,1024]{1,0:T(8,128)(2,1)} %bitcast.78), custom_call_target="tpu_custom_call" | custom-call | flops 4026531840 | bytes 10223616 | tf_op jit(solution)/shard_map/pallas_call | solution.py:200
  135.6 7.0 %all-to-all-start.4 = ((bf16[8,96,1024]{2,1,0:T(8,128)(2,1)}), bf16[8,96,1024]{2,1,0:T(8,128)(2,1)S(1)}, u32[]{:S(2)}, u32[]{:S(2)}) async-start(bf16[8,96,1024]{2,1,0:T(8,128)(2,1)} %bitcast.68), calls=%async_computation.4 | async-start | bytes 3145728 | tf_op jit(solution)/shard_map/all_to_all | solution.py:308
  142.8 10.0 %shard_map.134 = (bf16[2,1536,256]{2,1,0:T(8,128)(2,1)}, f32[2,1536,256]{2,1,0:T(8,128)}) custom-call(s32[1]{0:T(128)} %bitcast.15.core_ref, bf16[448,2048]{1,0:T(8,128)(2,1)} %bitcast.66, bf16[448,2048]{1,0:T(8,128)(2,1)} %bitcast.67, bf16[448,1024]{1,0:T(8,128)(2,1)} %get-tuple-element.63.refs_2_, bf16[448,512]{1,0:T(8,128)(2,1)} %get-tuple-element.64.refs_3_, ...), custom_call_target="tpu_custom_call" | custom-call | flops 3825205248 | bytes 16777216 | tf_op jit(solution)/shard_map/pallas_call | solution.py:265
  152.7 11.0 %all-to-all-done.4 = bf16[8,96,1024]{2,1,0:T(8,128)(2,1)S(1)} async-done(((bf16[8,96,1024]{2,1,0:T(8,128)(2,1)}), bf16[8,96,1024]{2,1,0:T(8,128)(2,1)S(1)}, u32[]{:S(2)}, u32[]{:S(2)}) %all-to-all-start.4) | async-done | bytes 1572896 | tf_op jit(solution)/shard_map/all_to_all | solution.py:308
  163.8 2.8 %fusion.30 = (bf16[640,1024]{1,0:T(8,128)(2,1)S(1)}, f32[640,1024]{1,0:T(8,128)}) fusion(bf16[8,96,1024]{2,1,0:T(8,128)(2,1)S(1)} %all-to-all-done.4, f32[8,640]{1,0:T(8,128)S(1)} %pad_maximum_fusion.2, f32[96]{0:T(128)S(1)} %iota_convert_fusion), kind=kOutput, calls=%fused_computation.68 | convolution fusion | flops 1007779840 | bytes 5525888 | tf_op jit(solution)/shard_map/dot_general | solution.py:24
  166.8 2.7 %collective-permute-start.18 = (bf16[128,512]{1,0:T(8,128)(2,1)S(1)}, bf16[128,512]{1,0:T(8,128)(2,1)S(1)}, u32[]{:S(2)}, u32[]{:S(2)}) collective-permute-start(bf16[128,512]{1,0:T(8,128)(2,1)S(1)} %get-tuple-element.84), channel_id=1, source_target_pairs={{0,7},{1,0},{2,1},{3,2},{4,3},{5,4},{6,5},{7,6},{8,15},{9,8},{10,9... | collective-permute-start | bytes 393224 | tf_op jit(solution)/shard_map/ppermute | solution.py:32
  172.9 2.7 %collective-permute-start.19 = (bf16[128,1024]{1,0:T(8,128)(2,1)S(1)}, bf16[128,1024]{1,0:T(8,128)(2,1)S(1)}, u32[]{:S(2)}, u32[]{:S(2)}) collective-permute-start(bf16[128,1024]{1,0:T(8,128)(2,1)S(1)} %pad_maximum_fusion.1), channel_id=1, source_target_pairs={{0,7},{1,0},{2,1},{3,2},{4,3},{5,4},{6,5},{7,6},{8,15},{9,8},{10,9... | collective-permute-start | bytes 786440 | tf_op jit(solution)/shard_map/ppermute | solution.py:32
  176.1 2.9 %collective-permute-done.19 = bf16[128,1024]{1,0:T(8,128)(2,1)S(1)} collective-permute-done((bf16[128,1024]{1,0:T(8,128)(2,1)S(1)}, bf16[128,1024]{1,0:T(8,128)(2,1)S(1)}, u32[]{:S(2)}, u32[]{:S(2)}) %collective-permute-start.19) | collective-permute-done | bytes 262176 | tf_op jit(solution)/shard_map/ppermute | solution.py:32
  179.0 3.2 %collective-permute-done.15 = bf16[128,1024]{1,0:T(8,128)(2,1)S(1)} collective-permute-done((bf16[128,1024]{1,0:T(8,128)(2,1)S(1)}, bf16[128,1024]{1,0:T(8,128)(2,1)S(1)}, u32[]{:S(2)}, u32[]{:S(2)}) %collective-permute-start.15) | collective-permute-done | bytes 262176 | tf_op jit(solution)/shard_map/ppermute | solution.py:32
  183.7 2.7 %collective-permute-start.20 = (bf16[128,1024]{1,0:T(8,128)(2,1)S(1)}, bf16[128,1024]{1,0:T(8,128)(2,1)S(1)}, u32[]{:S(2)}, u32[]{:S(2)}) collective-permute-start(bf16[128,1024]{1,0:T(8,128)(2,1)S(1)} %get-tuple-element.76), channel_id=1, source_target_pairs={{0,7},{1,0},{2,1},{3,2},{4,3},{5,4},{6,5},{7,6},{8,15},{9,8},{10,9... | collective-permute-start | bytes 786440 | tf_op jit(solution)/shard_map/ppermute | solution.py:32
  188.4 5.8 %collective-permute-start.29 = (bf16[2,1536,256]{2,1,0:T(8,128)(2,1)S(1)}, bf16[2,1536,256]{2,1,0:T(8,128)(2,1)S(1)}, u32[]{:S(2)}, u32[]{:S(2)}) collective-permute-start(bf16[2,1536,256]{2,1,0:T(8,128)(2,1)S(1)} %copy-done.15), channel_id=1, source_target_pairs={{0,64},{64,0},{1,65},{65,1},{2,66},{66,2},{3,67},{67,3},{4,68},{68... | collective-permute-start | bytes 4718600 | tf_op jit(solution)/shard_map/ppermute | solution.py:36
  194.4 2.7 %collective-permute-start.21 = (bf16[128,1024]{1,0:T(8,128)(2,1)S(1)}, bf16[128,1024]{1,0:T(8,128)(2,1)S(1)}, u32[]{:S(2)}, u32[]{:S(2)}) collective-permute-start(bf16[128,1024]{1,0:T(8,128)(2,1)S(1)} %get-tuple-element.82), channel_id=1, source_target_pairs={{0,7},{1,0},{2,1},{3,2},{4,3},{5,4},{6,5},{7,6},{8,15},{9,8},{10,9... | collective-permute-start | bytes 786440 | tf_op jit(solution)/shard_map/ppermute | solution.py:32
  197.2 4.0 %collective-permute-done.17 = bf16[128,1024]{1,0:T(8,128)(2,1)S(1)} collective-permute-done((bf16[128,1024]{1,0:T(8,128)(2,1)S(1)}, bf16[128,1024]{1,0:T(8,128)(2,1)S(1)}, u32[]{:S(2)}, u32[]{:S(2)}) %collective-permute-start.17) | collective-permute-done | bytes 262176 | tf_op jit(solution)/shard_map/ppermute | solution.py:32
  204.5 4.0 %collective-permute-start.22 = (bf16[128,1024]{1,0:T(8,128)(2,1)S(1)}, bf16[128,1024]{1,0:T(8,128)(2,1)S(1)}, u32[]{:S(2)}, u32[]{:S(2)}) collective-permute-start(bf16[128,1024]{1,0:T(8,128)(2,1)S(1)} %get-tuple-element.74), channel_id=1, source_target_pairs={{0,64},{64,0},{1,65},{65,1},{2,66},{66,2},{3,67},{67,3},{4,68},{68... | collective-permute-start | bytes 786440 | tf_op jit(solution)/shard_map/ppermute | solution.py:36
  208.6 6.3 %collective-permute-start.28 = (bf16[128,1024]{1,0:T(8,128)(2,1)S(1)}, bf16[128,1024]{1,0:T(8,128)(2,1)S(1)}, u32[]{:S(2)}, u32[]{:S(2)}) collective-permute-start(bf16[128,1024]{1,0:T(8,128)(2,1)S(1)} %collective-permute-done.27), channel_id=1, source_target_pairs={{0,64},{64,0},{1,65},{65,1},{2,66},{66,2},{3,67},{67,3},{4,68},{68... | collective-permute-start | bytes 786440 | tf_op jit(solution)/shard_map/ppermute | solution.py:36
  220.8 4.7 %all-to-all-start.5 = ((bf16[32,8,1024]{2,1,0:T(8,128)(2,1)}), bf16[32,8,1024]{2,1,0:T(8,128)(2,1)}, u32[]{:S(2)}, u32[]{:S(2)}) async-start(bf16[32,8,1024]{2,1,0:T(8,128)(2,1)} %fusion.5), calls=%async_computation.5 | async-start | bytes 1048576 | tf_op jit(solution)/shard_map/all_to_all | solution.py:359
  225.5 13.1 %collective-permute-done.30 = bf16[1536,256]{1,0:T(8,128)(2,1)} collective-permute-done((bf16[1536,256]{1,0:T(8,128)(2,1)}, bf16[1536,256]{1,0:T(8,128)(2,1)}, u32[]{:S(2)}, u32[]{:S(2)}) %collective-permute-start.30) | collective-permute-done | bytes 786464 | tf_op jit(solution)/shard_map/ppermute | solution.py:36
  (144 shorter events, 44.2 us)
Async XLA Ops:
  2.6 17.2 %collective-permute-start.3 = (bf16[128,1152]{1,0:T(8,128)(2,1)}, bf16[128,1152]{1,0:T(8,128)(2,1)S(1)}, u32[]{:S(2)}, u32[]{:S(2)}) collective-permute-start(bf16[128,1152]{1,0:T(8,128)(2,1)} %get-tuple-element.40.refs_1_), channel_id=1, source_target_pairs={{0,7},{1,0},{2,1},{3,2},{4,3},{5,4},{6,5},{7,6},{8,15},{9,8},{10,9... | collective-permute-start | bytes 884744 | tf_op jit(solution)/shard_map/ppermute | solution.py:32
  9.0 13.9 %collective-permute-start.1 = (bf16[128,1152]{1,0:T(8,128)(2,1)}, bf16[128,1152]{1,0:T(8,128)(2,1)S(1)}, u32[]{:S(2)}, u32[]{:S(2)}) collective-permute-start(bf16[128,1152]{1,0:T(8,128)(2,1)} %get-tuple-element.40.refs_1_), channel_id=1, source_target_pairs={{0,1},{1,2},{2,3},{3,4},{4,5},{5,6},{6,7},{7,0},{8,9},{9,10},{10,1... | collective-permute-start | bytes 884744 | tf_op jit(solution)/shard_map/ppermute | solution.py:32
  9.0 13.9 %collective-permute-start.2 = (bf16[128,1024]{1,0:T(8,128)(2,1)}, bf16[128,1024]{1,0:T(8,128)(2,1)S(1)}, u32[]{:S(2)}, u32[]{:S(2)}) collective-permute-start(bf16[128,1024]{1,0:T(8,128)(2,1)} %get-tuple-element.39.refs_0_), channel_id=1, source_target_pairs={{0,7},{1,0},{2,1},{3,2},{4,3},{5,4},{6,5},{7,6},{8,15},{9,8},{10,9... | collective-permute-start | bytes 786440 | tf_op jit(solution)/shard_map/ppermute | solution.py:32
  11.7 13.9 %collective-permute-start = (bf16[128,1024]{1,0:T(8,128)(2,1)}, bf16[128,1024]{1,0:T(8,128)(2,1)S(1)}, u32[]{:S(2)}, u32[]{:S(2)}) collective-permute-start(bf16[128,1024]{1,0:T(8,128)(2,1)} %get-tuple-element.39.refs_0_), channel_id=1, source_target_pairs={{0,1},{1,2},{2,3},{3,4},{4,5},{5,6},{6,7},{7,0},{8,9},{9,10},{10,1... | collective-permute-start | bytes 786440 | tf_op jit(solution)/shard_map/ppermute | solution.py:32
  13.9 18.9 %all-to-all-start = ((bf16[8,128,256]{1,2,0:T(8,128)(2,1)}), bf16[8,128,256]{1,2,0:T(8,128)(2,1)S(1)}, u32[]{:S(2)}, u32[]{:S(2)}) async-start(bf16[8,128,256]{1,2,0:T(8,128)(2,1)} %bitcast.6), calls=%async_computation | async-start | bytes 1048576 | tf_op jit(solution)/shard_map/all_to_all | solution.py:295
  19.9 18.2 %collective-permute-start.7 = (bf16[128,1152]{1,0:T(8,128)(2,1)S(1)}, bf16[128,1152]{1,0:T(8,128)(2,1)S(1)}, u32[]{:S(2)}, u32[]{:S(2)}) collective-permute-start(bf16[128,1152]{1,0:T(8,128)(2,1)S(1)} %collective-permute-done.3.refs_5_), channel_id=1, source_target_pairs={{0,7},{1,0},{2,1},{3,2},{4,3},{5,4},{6,5},{7,6},{8,15},{9,8},{10,9... | collective-permute-start | bytes 884744 | tf_op jit(solution)/shard_map/ppermute | solution.py:32
  22.9 15.1 %collective-permute-start.5 = (bf16[128,1152]{1,0:T(8,128)(2,1)S(1)}, bf16[128,1152]{1,0:T(8,128)(2,1)S(1)}, u32[]{:S(2)}, u32[]{:S(2)}) collective-permute-start(bf16[128,1152]{1,0:T(8,128)(2,1)S(1)} %collective-permute-done.1.refs_3_), channel_id=1, source_target_pairs={{0,1},{1,2},{2,3},{3,4},{4,5},{5,6},{6,7},{7,0},{8,9},{9,10},{10,1... | collective-permute-start | bytes 884744 | tf_op jit(solution)/shard_map/ppermute | solution.py:32
  22.9 12.0 %collective-permute-start.6 = (bf16[128,1024]{1,0:T(8,128)(2,1)S(1)}, bf16[128,1024]{1,0:T(8,128)(2,1)S(1)}, u32[]{:S(2)}, u32[]{:S(2)}) collective-permute-start(bf16[128,1024]{1,0:T(8,128)(2,1)S(1)} %collective-permute-done.2.refs_4_), channel_id=1, source_target_pairs={{0,7},{1,0},{2,1},{3,2},{4,3},{5,4},{6,5},{7,6},{8,15},{9,8},{10,9... | collective-permute-start | bytes 786440 | tf_op jit(solution)/shard_map/ppermute | solution.py:32
  25.6 12.4 %collective-permute-start.4 = (bf16[128,1024]{1,0:T(8,128)(2,1)S(1)}, bf16[128,1024]{1,0:T(8,128)(2,1)S(1)}, u32[]{:S(2)}, u32[]{:S(2)}) collective-permute-start(bf16[128,1024]{1,0:T(8,128)(2,1)S(1)} %collective-permute-done.refs_2_), channel_id=1, source_target_pairs={{0,1},{1,2},{2,3},{3,4},{4,5},{5,6},{6,7},{7,0},{8,9},{9,10},{10,1... | collective-permute-start | bytes 786440 | tf_op jit(solution)/shard_map/ppermute | solution.py:32
  38.1 34.5 %all-to-all-start.1 = ((bf16[8,56,2048]{2,1,0:T(8,128)(2,1)}), bf16[8,56,2048]{2,1,0:T(8,128)(2,1)S(1)}, u32[]{:S(2)}, u32[]{:S(2)}) async-start(bf16[8,56,2048]{2,1,0:T(8,128)(2,1)} %get-tuple-element.43), calls=%async_computation.1 | async-start | bytes 3670016 | tf_op jit(solution)/shard_map/all_to_all | solution.py:308
  44.3 6.7 %collective-permute-start.9 = (bf16[128,1152]{1,0:T(8,128)(2,1)S(1)}, bf16[128,1152]{1,0:T(8,128)(2,1)S(1)}, u32[]{:S(2)}, u32[]{:S(2)}) collective-permute-start(bf16[128,1152]{1,0:T(8,128)(2,1)S(1)} %collective-permute-done.7.refs_3_), channel_id=1, source_target_pairs={{0,7},{1,0},{2,1},{3,2},{4,3},{5,4},{6,5},{7,6},{8,15},{9,8},{10,9... | collective-permute-start | bytes 884744 | tf_op jit(solution)/shard_map/ppermute | solution.py:32
  44.6 8.2 %collective-permute-start.10 = (bf16[128,1024]{1,0:T(8,128)(2,1)S(1)}, bf16[128,1024]{1,0:T(8,128)(2,1)S(1)}, u32[]{:S(2)}, u32[]{:S(2)}) collective-permute-start(bf16[128,1024]{1,0:T(8,128)(2,1)S(1)} %collective-permute-done.4.refs_0_), channel_id=1, source_target_pairs={{0,1},{1,2},{2,3},{3,4},{4,5},{5,6},{6,7},{7,0},{8,9},{9,10},{10,1... | collective-permute-start | bytes 786440 | tf_op jit(solution)/shard_map/ppermute | solution.py:32
  45.8 12.4 %collective-permute-start.11 = (bf16[128,1152]{1,0:T(8,128)(2,1)S(1)}, bf16[128,1152]{1,0:T(8,128)(2,1)S(1)}, u32[]{:S(2)}, u32[]{:S(2)}) collective-permute-start(bf16[128,1152]{1,0:T(8,128)(2,1)S(1)} %collective-permute-done.5.refs_1_), channel_id=1, source_target_pairs={{0,1},{1,2},{2,3},{3,4},{4,5},{5,6},{6,7},{7,0},{8,9},{9,10},{10,1... | collective-permute-start | bytes 884744 | tf_op jit(solution)/shard_map/ppermute | solution.py:32
  45.8 10.8 %collective-permute-start.8 = (bf16[128,1024]{1,0:T(8,128)(2,1)S(1)}, bf16[128,1024]{1,0:T(8,128)(2,1)S(1)}, u32[]{:S(2)}, u32[]{:S(2)}) collective-permute-start(bf16[128,1024]{1,0:T(8,128)(2,1)S(1)} %collective-permute-done.6.refs_2_), channel_id=1, source_target_pairs={{0,7},{1,0},{2,1},{3,2},{4,3},{5,4},{6,5},{7,6},{8,15},{9,8},{10,9... | collective-permute-start | bytes 786440 | tf_op jit(solution)/shard_map/ppermute | solution.py:32
  51.0 15.3 %collective-permute-start.13 = (bf16[128,1152]{1,0:T(8,128)(2,1)S(1)}, bf16[128,1152]{1,0:T(8,128)(2,1)S(1)}, u32[]{:S(2)}, u32[]{:S(2)}) collective-permute-start(bf16[128,1152]{1,0:T(8,128)(2,1)S(1)} %collective-permute-done.9.refs_7_.refs_1_), channel_id=1, source_target_pairs={{0,7},{1,0},{2,1},{3,2},{4,3},{5,4},{6,5},{7,6},{8,15},{9,8},{10,9... | collective-permute-start | bytes 884744 | tf_op jit(solution)/shard_map/ppermute | solution.py:32
  52.9 13.4 %collective-permute-start.12 = (bf16[128,1024]{1,0:T(8,128)(2,1)S(1)}, bf16[128,1024]{1,0:T(8,128)(2,1)S(1)}, u32[]{:S(2)}, u32[]{:S(2)}) collective-permute-start(bf16[128,1024]{1,0:T(8,128)(2,1)S(1)} %collective-permute-done.10.refs_4_), channel_id=1, source_target_pairs={{0,1},{1,2},{2,3},{3,4},{4,5},{5,6},{6,7},{7,0},{8,9},{9,10},{10,1... | collective-permute-start | bytes 786440 | tf_op jit(solution)/shard_map/ppermute | solution.py:32
  73.9 46.7 %all-to-all-start.2 = ((bf16[8,96,2048]{2,1,0:T(8,128)(2,1)}), bf16[8,96,2048]{2,1,0:T(8,128)(2,1)S(1)}, u32[]{:S(2)}, u32[]{:S(2)}) async-start(bf16[8,96,2048]{2,1,0:T(8,128)(2,1)} %get-tuple-element.55), calls=%async_computation.2 | async-start | bytes 6291456 | tf_op jit(solution)/shard_map/all_to_all | solution.py:308
  120.6 14.9 %all-to-all-start.3 = ((bf16[8,56,1024]{2,1,0:T(8,128)(2,1)}), bf16[8,56,1024]{2,1,0:T(8,128)(2,1)}, u32[]{:S(2)}, u32[]{:S(2)}) async-start(bf16[8,56,1024]{2,1,0:T(8,128)(2,1)} %bitcast.69), calls=%async_computation.3 | async-start | bytes 1835008 | tf_op jit(solution)/shard_map/all_to_all | solution.py:308
  135.6 28.2 %all-to-all-start.4 = ((bf16[8,96,1024]{2,1,0:T(8,128)(2,1)}), bf16[8,96,1024]{2,1,0:T(8,128)(2,1)S(1)}, u32[]{:S(2)}, u32[]{:S(2)}) async-start(bf16[8,96,1024]{2,1,0:T(8,128)(2,1)} %bitcast.68), calls=%async_computation.4 | async-start | bytes 3145728 | tf_op jit(solution)/shard_map/all_to_all | solution.py:308
  175.7 6.5 %collective-permute-start.15 = (bf16[128,1024]{1,0:T(8,128)(2,1)S(1)}, bf16[128,1024]{1,0:T(8,128)(2,1)S(1)}, u32[]{:S(2)}, u32[]{:S(2)}) collective-permute-start(bf16[128,1024]{1,0:T(8,128)(2,1)S(1)} %pad_maximum_fusion), channel_id=1, source_target_pairs={{0,1},{1,2},{2,3},{3,4},{4,5},{5,6},{6,7},{7,0},{8,9},{9,10},{10,1... | collective-permute-start | bytes 786440 | tf_op jit(solution)/shard_map/ppermute | solution.py:32
  183.6 10.6 %collective-permute-start.16 = (bf16[128,1024]{1,0:T(8,128)(2,1)S(1)}, bf16[128,1024]{1,0:T(8,128)(2,1)S(1)}, u32[]{:S(2)}, u32[]{:S(2)}) collective-permute-start(bf16[128,1024]{1,0:T(8,128)(2,1)S(1)} %get-tuple-element.75), channel_id=1, source_target_pairs={{0,1},{1,2},{2,3},{3,4},{4,5},{5,6},{6,7},{7,0},{8,9},{9,10},{10,1... | collective-permute-start | bytes 786440 | tf_op jit(solution)/shard_map/ppermute | solution.py:32
  183.7 10.5 %collective-permute-start.20 = (bf16[128,1024]{1,0:T(8,128)(2,1)S(1)}, bf16[128,1024]{1,0:T(8,128)(2,1)S(1)}, u32[]{:S(2)}, u32[]{:S(2)}) collective-permute-start(bf16[128,1024]{1,0:T(8,128)(2,1)S(1)} %get-tuple-element.76), channel_id=1, source_target_pairs={{0,7},{1,0},{2,1},{3,2},{4,3},{5,4},{6,5},{7,6},{8,15},{9,8},{10,9... | collective-permute-start | bytes 786440 | tf_op jit(solution)/shard_map/ppermute | solution.py:32
  188.4 29.4 %collective-permute-start.29 = (bf16[2,1536,256]{2,1,0:T(8,128)(2,1)S(1)}, bf16[2,1536,256]{2,1,0:T(8,128)(2,1)S(1)}, u32[]{:S(2)}, u32[]{:S(2)}) collective-permute-start(bf16[2,1536,256]{2,1,0:T(8,128)(2,1)S(1)} %copy-done.15), channel_id=1, source_target_pairs={{0,64},{64,0},{1,65},{65,1},{2,66},{66,2},{3,67},{67,3},{4,68},{68... | collective-permute-start | bytes 4718600 | tf_op jit(solution)/shard_map/ppermute | solution.py:36
  194.3 6.9 %collective-permute-start.17 = (bf16[128,1024]{1,0:T(8,128)(2,1)S(1)}, bf16[128,1024]{1,0:T(8,128)(2,1)S(1)}, u32[]{:S(2)}, u32[]{:S(2)}) collective-permute-start(bf16[128,1024]{1,0:T(8,128)(2,1)S(1)} %get-tuple-element.81), channel_id=1, source_target_pairs={{0,1},{1,2},{2,3},{3,4},{4,5},{5,6},{6,7},{7,0},{8,9},{9,10},{10,1... | collective-permute-start | bytes 786440 | tf_op jit(solution)/shard_map/ppermute | solution.py:32
  194.4 6.8 %collective-permute-start.21 = (bf16[128,1024]{1,0:T(8,128)(2,1)S(1)}, bf16[128,1024]{1,0:T(8,128)(2,1)S(1)}, u32[]{:S(2)}, u32[]{:S(2)}) collective-permute-start(bf16[128,1024]{1,0:T(8,128)(2,1)S(1)} %get-tuple-element.82), channel_id=1, source_target_pairs={{0,7},{1,0},{2,1},{3,2},{4,3},{5,4},{6,5},{7,6},{8,15},{9,8},{10,9... | collective-permute-start | bytes 786440 | tf_op jit(solution)/shard_map/ppermute | solution.py:32
  201.7 6.9 %collective-permute-start.27 = (bf16[128,1024]{1,0:T(8,128)(2,1)S(1)}, bf16[128,1024]{1,0:T(8,128)(2,1)S(1)}, u32[]{:S(2)}, u32[]{:S(2)}) collective-permute-start(bf16[128,1024]{1,0:T(8,128)(2,1)S(1)} %get-tuple-element.74), channel_id=1, source_target_pairs={{0,8},{128,136},{8,0},{136,128},{1,9},{129,137},{9,1},{137,129},{2... | collective-permute-start | bytes 786440 | tf_op jit(solution)/shard_map/ppermute | solution.py:349
  203.0 11.9 %collective-permute-start.25 = (bf16[128,1024]{1,0:T(8,128)(2,1)S(1)}, bf16[128,1024]{1,0:T(8,128)(2,1)S(1)}, u32[]{:S(2)}, u32[]{:S(2)}) collective-permute-start(bf16[128,1024]{1,0:T(8,128)(2,1)S(1)} %get-tuple-element.74), channel_id=1, source_target_pairs={{0,136},{128,0},{8,128},{136,8},{1,137},{129,1},{9,129},{137,9},{2... | collective-permute-start | bytes 786440 | tf_op jit(solution)/shard_map/ppermute | solution.py:349
  204.5 11.7 %collective-permute-start.23 = (bf16[128,1024]{1,0:T(8,128)(2,1)S(1)}, bf16[128,1024]{1,0:T(8,128)(2,1)S(1)}, u32[]{:S(2)}, u32[]{:S(2)}) collective-permute-start(bf16[128,1024]{1,0:T(8,128)(2,1)S(1)} %get-tuple-element.74), channel_id=1, source_target_pairs={{0,128},{128,8},{8,136},{136,0},{1,129},{129,9},{9,137},{137,1},{2... | collective-permute-start | bytes 786440 | tf_op jit(solution)/shard_map/ppermute | solution.py:349
  204.5 13.2 %collective-permute-start.22 = (bf16[128,1024]{1,0:T(8,128)(2,1)S(1)}, bf16[128,1024]{1,0:T(8,128)(2,1)S(1)}, u32[]{:S(2)}, u32[]{:S(2)}) collective-permute-start(bf16[128,1024]{1,0:T(8,128)(2,1)S(1)} %get-tuple-element.74), channel_id=1, source_target_pairs={{0,64},{64,0},{1,65},{65,1},{2,66},{66,2},{3,67},{67,3},{4,68},{68... | collective-permute-start | bytes 786440 | tf_op jit(solution)/shard_map/ppermute | solution.py:36
  208.6 10.6 %collective-permute-start.28 = (bf16[128,1024]{1,0:T(8,128)(2,1)S(1)}, bf16[128,1024]{1,0:T(8,128)(2,1)S(1)}, u32[]{:S(2)}, u32[]{:S(2)}) collective-permute-start(bf16[128,1024]{1,0:T(8,128)(2,1)S(1)} %collective-permute-done.27), channel_id=1, source_target_pairs={{0,64},{64,0},{1,65},{65,1},{2,66},{66,2},{3,67},{67,3},{4,68},{68... | collective-permute-start | bytes 786440 | tf_op jit(solution)/shard_map/ppermute | solution.py:36
  219.1 19.5 %collective-permute-start.30 = (bf16[1536,256]{1,0:T(8,128)(2,1)}, bf16[1536,256]{1,0:T(8,128)(2,1)}, u32[]{:S(2)}, u32[]{:S(2)}) collective-permute-start(bf16[1536,256]{1,0:T(8,128)(2,1)} %fusion.8), channel_id=1, source_target_pairs={{0,128},{128,0},{1,129},{129,1},{2,130},{130,2},{3,131},{131,3},{4... | collective-permute-start | bytes 2359304 | tf_op jit(solution)/shard_map/ppermute | solution.py:36
  220.8 20.9 %all-to-all-start.5 = ((bf16[32,8,1024]{2,1,0:T(8,128)(2,1)}), bf16[32,8,1024]{2,1,0:T(8,128)(2,1)}, u32[]{:S(2)}, u32[]{:S(2)}) async-start(bf16[32,8,1024]{2,1,0:T(8,128)(2,1)} %fusion.5), calls=%async_computation.5 | async-start | bytes 1048576 | tf_op jit(solution)/shard_map/all_to_all | solution.py:359
  (32 other events, 286.9 us)

commit v2 on v1

--- a/solution.py
+++ b/solution.py
@@ -44,20 +44,19 @@
     return pairs
 
 
-def ring_scatter(blocks):
+def ring_scatter(blocks, later):
     half = blocks[4].shape[1] // 2
     far = blocks[4].astype(bf16)
     got = shift_z(far[:, :half], 1).astype(f32)
     right = jnp.concatenate([blocks[3][:, :half] + got, blocks[3][:, half:]], axis=1)
     got = shift_z(far[:, half:], -1).astype(f32)
     left = jnp.concatenate([blocks[-3][:, :half], blocks[-3][:, half:] + got], axis=1)
-    for d in (2, 1, 0):
-        got_right = shift_z(right.astype(bf16), 1).astype(f32)
-        got_left = shift_z(left.astype(bf16), -1).astype(f32)
-        if d:
-            right = blocks[d] + got_right
-            left = blocks[-d] + got_left
-    return blocks[0] + got_right + got_left
+    for d in (2, 1):
+        right = blocks[d] + shift_z(right.astype(bf16), 1).astype(f32)
+        left = blocks[-d] + shift_z(left.astype(bf16), -1).astype(f32)
+    right, left, later = lax.optimization_barrier((right.astype(bf16), left.astype(bf16), later))
+    right, left = shift_z(right, 1), shift_z(left, -1)
+    return blocks[0] + right.astype(f32) + left.astype(f32), later
 
 
 def enter_kernel(resid_ref, grad_ref, gain_ref, ids_ref, vals_ref, in_ref, out_ref):
@@ -126,15 +125,16 @@
             target_ref[:, lines] = place
             gates[:, lines] = gate
 
-    e = pl.program_id(0)
     row_ids = (lax.broadcasted_iota(jnp.int32, (rows, held.shape[0]), 0) + offset).astype(f32)
-    hit = row_ids == target_ref[pl.ds(e, 1), :]
-    gate = jnp.sum(jnp.where(hit, gates[pl.ds(e, 1), :], 0.0), axis=1, keepdims=True)
-    onehot = jnp.where(hit, 1.0, 0.0).astype(bf16)
-    picked = jnp.dot(onehot, held[:, :half], preferred_element_type=f32)
-    out_ref[0, :, :half] = picked.astype(bf16)
-    picked = jnp.dot(onehot, held[:, half:], preferred_element_type=f32)
-    out_ref[0, :, half:] = (picked * gate).astype(bf16)
+    for i in range(out_ref.shape[0]):
+        e = pl.program_id(0) * out_ref.shape[0] + i
+        hit = row_ids == target_ref[pl.ds(e, 1), :]
+        gate = jnp.sum(jnp.where(hit, gates[pl.ds(e, 1), :], 0.0), axis=1, keepdims=True)
+        onehot = jnp.where(hit, 1.0, 0.0).astype(bf16)
+        picked = jnp.dot(onehot, held[:, :half], preferred_element_type=f32)
+        out_ref[i, :, :half] = picked.astype(bf16)
+        picked = jnp.dot(onehot, held[:, half:], preferred_element_type=f32)
+        out_ref[i, :, half:] = (picked * gate).astype(bf16)
 
 
 def pick_rows(z, blocks, width, total, first=0, rows=None, into=None):
@@ -149,10 +149,10 @@
         functools.partial(pick_kernel, layout, first, total - rows),
         grid_spec=pltpu.PrefetchScalarGridSpec(
             num_scalar_prefetch=1,
-            grid=(PLANE,),
+            grid=(2,),
             in_specs=whole + [pl.BlockSpec(memory_space=pl.ANY)] * (into is not None),
             out_specs=[
-                pl.BlockSpec((1, rows, width), lambda e, z: (e, at, 0)),
+                pl.BlockSpec((PLANE // 2, rows, width), lambda e, z: (e, at, 0)),
                 pl.BlockSpec((PLANE, count * tokens), lambda e, z: (0, 0)),
             ],
             scratch_shapes=[
@@ -242,7 +242,7 @@
         mine_ref[0, feature:, :] = low
 
 
-def weight_terms(core, near, far):
+def weight_terms(ylo, core, near, far):
     specs, arrays, flops = [], [], 0
     for got, slopes, hidden in (near, far):
         rows, width = got.shape
@@ -251,7 +251,7 @@
         share = feature // 4
 
         def block(s, core):
-            return (s % 2) * 2 + jnp.where(s < 2, 1 - core[0], core[0])
+            return jnp.where(s % 2 == 0, 1 - core[1], core[1]) * 2 + jnp.where(s < 2, 1 - core[0], core[0])
 
         specs += [
             pl.BlockSpec((rows, feature), lambda s, core: (0, 0)),
@@ -276,7 +276,7 @@
         out_shape=[jax.ShapeDtypeStruct(shape, bf16), jax.ShapeDtypeStruct(shape, f32)],
         compiler_params=pltpu.CompilerParams(vmem_limit_bytes=56 << 20),
         cost_estimate=pl.CostEstimate(flops=flops, bytes_accessed=16 << 20, transcendentals=0),
-    )(core.reshape(1), *arrays)
+    )(jnp.stack([core, ylo]), *arrays)
 
 
 def body(attn_out, resid, out_grad, gain, expert_ids, gate_vals, w_gate, w_up, w_down):
@@ -313,18 +313,11 @@
     back_near, *saved_near = run_expert(got_near, w_gate, w_up, w_down, 2)
     back_near, got_far = lax.optimization_barrier((back_near, got_far))
     returned_near = over_plane(back_near.reshape(PLANE, -1, feature))
-    back_far, *saved_far = run_expert(got_far, w_gate, w_up, w_down, 3)
+    back_far, *saved_far = run_expert(got_far, w_gate, w_up, w_down, 2)
     returned_near, back_far = lax.optimization_barrier((returned_near, back_far))
     returned_far = over_plane(back_far.reshape(PLANE, -1, feature))
-    other, own = weight_terms(core, (got_near, *saved_near), (got_far, *saved_far))
+    other, own = weight_terms(ylo, core, (got_near, *saved_near), (got_far, *saved_far))
     returned_far, other, own = lax.optimization_barrier((returned_far, other, own))
-
-    total = own + swap(other, "core").astype(f32)
-    held = lax.dynamic_index_in_dim(total, ylo, 0, keepdims=False)
-    other = lax.dynamic_index_in_dim(total, 1 - ylo, 0, keepdims=False)
-    total = held + swap(other.astype(bf16), "ylo").astype(f32)
-    half = total.shape[1] // 2
-    gate_out, up_out, down_out = total[None, :feature, :half], total[None, :feature, half:], total[None, feature:]
 
     terms = {}
     for target, deltas, returned in ((target_near, NEAR, returned_near), (target_far, FAR, returned_far)):
@@ -333,7 +326,10 @@
         term = contract_rows(pick.reshape(PLANE * rows, -1), returned.reshape(PLANE * rows, feature))
         for i, d in enumerate(deltas):
             terms[d] = term[i * tokens : (i + 1) * tokens]
-    d_moe = ring_scatter(terms)
+    d_moe, other = ring_scatter(terms, other)
+    from_core = swap(other, "core").astype(f32)
+    beside = (own[0] + from_core[0]).astype(bf16)
+
     gain_f = gain[None, :]
     resid_f = resid.astype(f32)
     inv_rms = lax.rsqrt(jnp.mean(resid_f * resid_f, axis=1, keepdims=True) + epsilon)
@@ -355,7 +351,11 @@
     part = contract_rows(
         jnp.concatenate([a for a, _ in pieces], axis=0), jnp.concatenate([b for _, b in pieces], axis=0)
     )
-    part = part.astype(bf16).reshape(32, 8, feature)
+    part, beside = lax.optimization_barrier((part.astype(bf16), beside))
+    total = own[1] + from_core[1] + swap(beside, "ylo").astype(f32)
+    half = total.shape[1] // 2
+    gate_out, up_out, down_out = total[None, :feature, :half], total[None, :feature, half:], total[None, feature:]
+    part = part.reshape(32, 8, feature)
     part = lax.all_to_all(part, ("x", "z"), split_axis=0, concat_axis=0, tiled=True)
     projection_grad = jnp.sum(part.astype(f32), axis=0)
     return (d_resid, projection_grad, gate_out, up_out, down_out)

time: 245 us -> 260 us (1.061); the launches traced: 243 us -> 255 us
  starting transfers between devices: 88 us -> 99.8 us
  waiting for transfers between devices: 86.3 us -> 90.2 us
  Pallas kernels: 45.8 us -> 41.9 us
    ppermute x22, starting transfers between devices: 31.9 us -> 40.7 us  [shift_z(): lax.ppermute(block, 'z', [(i, (i + step) % RING) for i in range(RING)])]
    pallas_call x3, Pallas kernels: 19.3 us -> 14.9 us  [pick_rows(): pl.pallas_call(functools.partial(pick_kernel, layout, first, total - rows...]
    ppermute x6, starting transfers between devices: 18.8 us -> 21.5 us  [swap(): return lax.ppermute(block, axis, [(0, 1), (1, 0)])]
  transfers between devices with their start and end apart: 37 -> 37, of which waited for: 13 -> 18; matrix products, arithmetic and copies ran while one was open for 5% -> 4% of each run, Pallas kernels for 18% -> 16%
where the time goes in v2:
time: 260 us; the launch traced here: 255 us
  starting transfers between devices  99.8 us (38%)
  waiting for transfers between devices  90.2 us (35%)
  Pallas kernels  41.9 us (16%)
  local copies, waits for them, and re-layouts  9.53 us (4%)
  other arithmetic  7.9 us (3%)
  matrix products  4.68 us (2%)
    all_to_all x4, waiting for transfers between devices, over_plane(): lax.all_to_all(rows, ('x', 'yhi'), split_axis=0, concat_axis=0, tiled=True)  47 us
    ppermute x22, starting transfers between devices, shift_z(): lax.ppermute(block, 'z', [(i, (i + step) % RING) for i in range(RING)])  40.7 us
    ppermute x22, waiting for transfers between devices, shift_z(): lax.ppermute(block, 'z', [(i, (i + step) % RING) for i in range(RING)])  27.3 us
    all_to_all x4, starting transfers between devices, over_plane(): lax.all_to_all(rows, ('x', 'yhi'), split_axis=0, concat_axis=0, tiled=True)  23.4 us
    ppermute x6, starting transfers between devices, swap(): return lax.ppermute(block, axis, [(0, 1), (1, 0)])  21.5 us
    ppermute x6, waiting for transfers between devices, swap(): return lax.ppermute(block, axis, [(0, 1), (1, 0)])  15.2 us
    pallas_call x3, Pallas kernels, pick_rows(): pl.pallas_call(functools.partial(pick_kernel, layout, first, total - rows...  14.9 us
    pallas_call x2, Pallas kernels, run_expert(): pl.pallas_call(expert_kernel, grid=(steps,), in_specs=[pl.BlockSpec((rows...  14.4 us
  transfers between devices with their start and end apart: 37, of which 18 were waited for; matrix products, arithmetic and copies ran while one was open for 4% of the time, Pallas kernels for 16%

profile of v2, /device:TPU:1, one launch (start us, length us, event | category | flops | bytes accessed | tf_op | source)
XLA Modules:
  0.0 255.3 jit_solution(3500467443396969063)
XLA Ops:
  2.6 6.4 %collective-permute-start.3 = (bf16[128,1152]{1,0:T(8,128)(2,1)}, bf16[128,1152]{1,0:T(8,128)(2,1)S(1)}, u32[]{:S(2)}, u32[]{:S(2)}) collective-permute-start(bf16[128,1152]{1,0:T(8,128)(2,1)} %get-tuple-element.45.refs_1_), channel_id=1, source_target_pairs={{0,7},{1,0},{2,1},{3,2},{4,3},{5,4},{6,5},{7,6},{8,15},{9,8},{10,9... | collective-permute-start | bytes 884744 | tf_op jit(solution)/shard_map/ppermute | solution.py:32
  9.0 2.7 %collective-permute-start.2 = (bf16[128,1024]{1,0:T(8,128)(2,1)}, bf16[128,1024]{1,0:T(8,128)(2,1)S(1)}, u32[]{:S(2)}, u32[]{:S(2)}) collective-permute-start(bf16[128,1024]{1,0:T(8,128)(2,1)} %get-tuple-element.44.refs_0_), channel_id=1, source_target_pairs={{0,7},{1,0},{2,1},{3,2},{4,3},{5,4},{6,5},{7,6},{8,15},{9,8},{10,9... | collective-permute-start | bytes 786440 | tf_op jit(solution)/shard_map/ppermute | solution.py:32
  13.9 6.0 %all-to-all-start = ((bf16[8,128,256]{1,2,0:T(8,128)(2,1)}), bf16[8,128,256]{1,2,0:T(8,128)(2,1)S(1)}, u32[]{:S(2)}, u32[]{:S(2)}) async-start(bf16[8,128,256]{1,2,0:T(8,128)(2,1)} %bitcast.6), calls=%async_computation | async-start | bytes 1048576 | tf_op jit(solution)/shard_map/all_to_all | solution.py:295
  19.9 3.0 %collective-permute-start.7 = (bf16[128,1152]{1,0:T(8,128)(2,1)S(1)}, bf16[128,1152]{1,0:T(8,128)(2,1)S(1)}, u32[]{:S(2)}, u32[]{:S(2)}) collective-permute-start(bf16[128,1152]{1,0:T(8,128)(2,1)S(1)} %collective-permute-done.3.refs_5_), channel_id=1, source_target_pairs={{0,7},{1,0},{2,1},{3,2},{4,3},{5,4},{6,5},{7,6},{8,15},{9,8},{10,9... | collective-permute-start | bytes 884744 | tf_op jit(solution)/shard_map/ppermute | solution.py:32
  22.9 2.7 %collective-permute-start.6 = (bf16[128,1024]{1,0:T(8,128)(2,1)S(1)}, bf16[128,1024]{1,0:T(8,128)(2,1)S(1)}, u32[]{:S(2)}, u32[]{:S(2)}) collective-permute-start(bf16[128,1024]{1,0:T(8,128)(2,1)S(1)} %collective-permute-done.2.refs_4_), channel_id=1, source_target_pairs={{0,7},{1,0},{2,1},{3,2},{4,3},{5,4},{6,5},{7,6},{8,15},{9,8},{10,9... | collective-permute-start | bytes 786440 | tf_op jit(solution)/shard_map/ppermute | solution.py:32
  26.3 5.1 %shard_map.129 = (bf16[8,56,2048]{2,1,0:T(8,128)(2,1)}, f32[8,384]{1,0:T(8,128)}) custom-call(s32[1]{0:T(128)} %bitcast.z_ref, bf16[128,1024]{1,0:T(8,128)(2,1)} %get-tuple-element.44.refs_0_, bf16[128,1152]{1,0:T(8,128)(2,1)} %get-tuple-element.45.refs_1_, bf16[128,1024]{1,0:T(8,128)(2,1)} %copy-done.24, bf16[128,1152]{1,0:T(8,128)(2,1)} %copy-done.20, ...), custom_call_target="tpu_custom_call" | custom-call | flops 704643072 | bytes 3407872 | tf_op jit(solution)/shard_map/pallas_call | solution.py:148
  31.4 3.6 %collective-permute-done.6.refs_2_ = bf16[128,1024]{1,0:T(8,128)(2,1)S(1)} collective-permute-done((bf16[128,1024]{1,0:T(8,128)(2,1)S(1)}, bf16[128,1024]{1,0:T(8,128)(2,1)S(1)}, u32[]{:S(2)}, u32[]{:S(2)}) %collective-permute-start.6) | collective-permute-done | bytes 262176 | tf_op jit(solution)/shard_map/ppermute | solution.py:32
  34.9 3.2 %collective-permute-done.4.refs_0_ = bf16[128,1024]{1,0:T(8,128)(2,1)} collective-permute-done((bf16[128,1024]{1,0:T(8,128)(2,1)S(1)}, bf16[128,1024]{1,0:T(8,128)(2,1)}, u32[]{:S(2)}, u32[]{:S(2)}) %collective-permute-start.4) | collective-permute-done | bytes 262176 | tf_op jit(solution)/shard_map/ppermute | solution.py:32
  38.2 6.2 %all-to-all-start.1 = ((bf16[8,56,2048]{2,1,0:T(8,128)(2,1)}), bf16[8,56,2048]{2,1,0:T(8,128)(2,1)S(1)}, u32[]{:S(2)}, u32[]{:S(2)}) async-start(bf16[8,56,2048]{2,1,0:T(8,128)(2,1)} %get-tuple-element.48), calls=%async_computation.1 | async-start | bytes 3670016 | tf_op jit(solution)/shard_map/all_to_all | solution.py:308
  53.1 3.6 %collective-permute-done.8.refs_6_.refs_0_ = bf16[128,1024]{1,0:T(8,128)(2,1)S(1)} collective-permute-done((bf16[128,1024]{1,0:T(8,128)(2,1)S(1)}, bf16[128,1024]{1,0:T(8,128)(2,1)S(1)}, u32[]{:S(2)}, u32[]{:S(2)}) %collective-permute-start.8) | collective-permute-done | bytes 262176 | tf_op jit(solution)/shard_map/ppermute | solution.py:32
  59.2 5.9 %shard_map.130 = (bf16[8,96,2048]{2,1,0:T(8,128)(2,1)}, f32[8,512]{1,0:T(8,128)}) custom-call(s32[1]{0:T(128)} %bitcast.z_ref, bf16[128,1024]{1,0:T(8,128)(2,1)} %collective-permute-done.4.refs_0_, bf16[128,1152]{1,0:T(8,128)(2,1)} %copy-done.18, bf16[128,1024]{1,0:T(8,128)(2,1)} %copy-done.22, bf16[128,1152]{1,0:T(8,128)(2,1)} %copy-done.17, ...), custom_call_target="tpu_custom_call" | custom-call | flops 1610612736 | bytes 5242880 | tf_op jit(solution)/shard_map/pallas_call | solution.py:148
  65.9 3.9 %shard_map.131 = (bf16[8,96,2048]{2,1,0:T(8,128)(2,1)}, f32[8,256]{1,0:T(8,128)}) custom-call(s32[1]{0:T(128)} %bitcast.z_ref, bf16[128,1024]{1,0:T(8,128)(2,1)} %copy-done.10, bf16[128,1152]{1,0:T(8,128)(2,1)} %copy-done.8, bf16[128,1024]{1,0:T(8,128)(2,1)} %copy-done.11, bf16[128,1152]{1,0:T(8,128)(2,1)} %copy-done.9, ...), custom_call_target="tpu_custom_call", output_to_operand_aliasing={{0}: (5, {})} | custom-call | flops 268435456 | bytes 2097152 | tf_op jit(solution)/shard_map/pallas_call | solution.py:148
  71.5 6.0 %all-to-all-start.2 = ((bf16[8,96,2048]{2,1,0:T(8,128)(2,1)}), bf16[8,96,2048]{2,1,0:T(8,128)(2,1)S(1)}, u32[]{:S(2)}, u32[]{:S(2)}) async-start(bf16[8,96,2048]{2,1,0:T(8,128)(2,1)} %get-tuple-element.60), calls=%async_computation.2 | async-start | bytes 6291456 | tf_op jit(solution)/shard_map/all_to_all | solution.py:308
  77.5 6.4 %shard_map.132 = (bf16[448,1024]{1,0:T(8,128)(2,1)}, bf16[448,1024]{1,0:T(8,128)(2,1)}, bf16[448,512]{1,0:T(8,128)(2,1)}) custom-call(bf16[448,2048]{1,0:T(8,128)(2,1)} %bitcast.67, bf16[1024,512]{1,0:T(8,128)(2,1)} %bitcast.76, bf16[1024,512]{1,0:T(8,128)(2,1)} %bitcast.78, bf16[512,1024]{1,0:T(8,128)(2,1)} %bitcast.80), custom_call_target="tpu_custom_call" | custom-call | flops 2348810240 | bytes 7274496 | tf_op jit(solution)/shard_map/pallas_call | solution.py:200
  83.9 34.0 %all-to-all-done.2 = bf16[8,96,2048]{2,1,0:T(8,128)(2,1)S(1)} async-done(((bf16[8,96,2048]{2,1,0:T(8,128)(2,1)}), bf16[8,96,2048]{2,1,0:T(8,128)(2,1)S(1)}, u32[]{:S(2)}, u32[]{:S(2)}) %all-to-all-start.2) | async-done | bytes 3145760 | tf_op jit(solution)/shard_map/all_to_all | solution.py:308
  117.9 4.2 %all-to-all-start.3 = ((bf16[8,56,1024]{2,1,0:T(8,128)(2,1)}), bf16[8,56,1024]{2,1,0:T(8,128)(2,1)}, u32[]{:S(2)}, u32[]{:S(2)}) async-start(bf16[8,56,1024]{2,1,0:T(8,128)(2,1)} %bitcast.71), calls=%async_computation.3 | async-start | bytes 1835008 | tf_op jit(solution)/shard_map/all_to_all | solution.py:308
  122.1 8.0 %shard_map.133 = (bf16[768,1024]{1,0:T(8,128)(2,1)}, bf16[768,1024]{1,0:T(8,128)(2,1)}, bf16[768,512]{1,0:T(8,128)(2,1)}) custom-call(bf16[768,2048]{1,0:T(8,128)(2,1)} %bitcast.55, bf16[1024,512]{1,0:T(8,128)(2,1)} %bitcast.77, bf16[1024,512]{1,0:T(8,128)(2,1)} %bitcast.79, bf16[512,1024]{1,0:T(8,128)(2,1)} %bitcast.81), custom_call_target="tpu_custom_call" | custom-call | flops 4026531840 | bytes 10223616 | tf_op jit(solution)/shard_map/pallas_call | solution.py:200
  130.1 2.7 %all-to-all-done.3 = bf16[8,56,1024]{2,1,0:T(8,128)(2,1)} async-done(((bf16[8,56,1024]{2,1,0:T(8,128)(2,1)}), bf16[8,56,1024]{2,1,0:T(8,128)(2,1)}, u32[]{:S(2)}, u32[]{:S(2)}) %all-to-all-start.3) | async-done | bytes 917536 | tf_op jit(solution)/shard_map/all_to_all | solution.py:308
  132.8 7.0 %all-to-all-start.4 = ((bf16[8,96,1024]{2,1,0:T(8,128)(2,1)}), bf16[8,96,1024]{2,1,0:T(8,128)(2,1)S(1)}, u32[]{:S(2)}, u32[]{:S(2)}) async-start(bf16[8,96,1024]{2,1,0:T(8,128)(2,1)} %bitcast.70), calls=%async_computation.4 | async-start | bytes 3145728 | tf_op jit(solution)/shard_map/all_to_all | solution.py:308
  140.5 10.6 %shard_map.134 = (bf16[2,1536,256]{2,1,0:T(8,128)(2,1)}, f32[2,1536,256]{2,1,0:T(8,128)}) custom-call(s32[2]{0:T(128)} %pad_add_fusion.core_ref, bf16[448,2048]{1,0:T(8,128)(2,1)} %bitcast.68, bf16[448,2048]{1,0:T(8,128)(2,1)} %bitcast.69, bf16[448,1024]{1,0:T(8,128)(2,1)} %get-tuple-element.68.refs_2_, bf16[448,512]{1,0:T(8,128)(2,1)} %get-tuple-element.69.refs_3_, ...), custom_call_target="tpu_custom_call" | custom-call | flops 3825205248 | bytes 16777216 | tf_op jit(solution)/shard_map/pallas_call | solution.py:265
  151.1 9.9 %all-to-all-done.4 = bf16[8,96,1024]{2,1,0:T(8,128)(2,1)S(1)} async-done(((bf16[8,96,1024]{2,1,0:T(8,128)(2,1)}), bf16[8,96,1024]{2,1,0:T(8,128)(2,1)S(1)}, u32[]{:S(2)}, u32[]{:S(2)}) %all-to-all-start.4) | async-done | bytes 1572896 | tf_op jit(solution)/shard_map/all_to_all | solution.py:308
  166.5 3.1 %collective-permute-done.14 = bf16[128,512]{1,0:T(8,128)(2,1)S(1)} collective-permute-done((bf16[128,512]{1,0:T(8,128)(2,1)S(1)}, bf16[128,512]{1,0:T(8,128)(2,1)S(1)}, u32[]{:S(2)}, u32[]{:S(2)}) %collective-permute-start.14) | collective-permute-done | bytes 131104 | tf_op jit(solution)/shard_map/ppermute | solution.py:32
  169.8 11.6 %collective-permute-start.18 = (bf16[128,1024]{1,0:T(8,128)(2,1)S(1)}, bf16[128,1024]{1,0:T(8,128)(2,1)S(1)}, u32[]{:S(2)}, u32[]{:S(2)}) collective-permute-start(bf16[128,1024]{1,0:T(8,128)(2,1)S(1)} %pad_maximum_fusion.1), channel_id=1, source_target_pairs={{0,7},{1,0},{2,1},{3,2},{4,3},{5,4},{6,5},{7,6},{8,15},{9,8},{10,9... | collective-permute-start | bytes 786440 | tf_op jit(solution)/shard_map/ppermute | solution.py:32
  181.5 3.3 %collective-permute-done.18 = bf16[128,1024]{1,0:T(8,128)(2,1)S(1)} collective-permute-done((bf16[128,1024]{1,0:T(8,128)(2,1)S(1)}, bf16[128,1024]{1,0:T(8,128)(2,1)S(1)}, u32[]{:S(2)}, u32[]{:S(2)}) %collective-permute-start.18) | collective-permute-done | bytes 262176 | tf_op jit(solution)/shard_map/ppermute | solution.py:32
  186.1 3.2 %collective-permute-start.19 = (bf16[128,1024]{1,0:T(8,128)(2,1)S(1)}, bf16[128,1024]{1,0:T(8,128)(2,1)S(1)}, u32[]{:S(2)}, u32[]{:S(2)}) collective-permute-start(bf16[128,1024]{1,0:T(8,128)(2,1)S(1)} %get-tuple-element.85), channel_id=1, source_target_pairs={{0,7},{1,0},{2,1},{3,2},{4,3},{5,4},{6,5},{7,6},{8,15},{9,8},{10,9... | collective-permute-start | bytes 786440 | tf_op jit(solution)/shard_map/ppermute | solution.py:32
  192.6 3.1 %collective-permute-done.16 = bf16[128,1024]{1,0:T(8,128)(2,1)S(1)} collective-permute-done((bf16[128,1024]{1,0:T(8,128)(2,1)S(1)}, bf16[128,1024]{1,0:T(8,128)(2,1)S(1)}, u32[]{:S(2)}, u32[]{:S(2)}) %collective-permute-start.16) | collective-permute-done | bytes 262176 | tf_op jit(solution)/shard_map/ppermute | solution.py:32
  195.9 2.7 %collective-permute-start.21 = (bf16[128,1024]{1,0:T(8,128)(2,1)S(1)}, bf16[128,1024]{1,0:T(8,128)(2,1)S(1)}, u32[]{:S(2)}, u32[]{:S(2)}) collective-permute-start(bf16[128,1024]{1,0:T(8,128)(2,1)S(1)} %get-tuple-element.77), channel_id=1, source_target_pairs={{0,7},{1,0},{2,1},{3,2},{4,3},{5,4},{6,5},{7,6},{8,15},{9,8},{10,9... | collective-permute-start | bytes 786440 | tf_op jit(solution)/shard_map/ppermute | solution.py:32
  198.7 8.9 %collective-permute-start.29 = (bf16[2,1536,256]{2,1,0:T(8,128)(2,1)S(1)}, bf16[2,1536,256]{2,1,0:T(8,128)(2,1)S(1)}, u32[]{:S(2)}, u32[]{:S(2)}) collective-permute-start(bf16[2,1536,256]{2,1,0:T(8,128)(2,1)S(1)} %copy-done.16), channel_id=1, source_target_pairs={{0,64},{64,0},{1,65},{65,1},{2,66},{66,2},{3,67},{67,3},{4,68},{68... | collective-permute-start | bytes 4718600 | tf_op jit(solution)/shard_map/ppermute | solution.py:36
  211.8 5.0 %collective-permute-start.22 = (bf16[128,1024]{1,0:T(8,128)(2,1)S(1)}, bf16[128,1024]{1,0:T(8,128)(2,1)S(1)}, u32[]{:S(2)}, u32[]{:S(2)}) collective-permute-start(bf16[128,1024]{1,0:T(8,128)(2,1)S(1)} %get-tuple-element.84), channel_id=1, source_target_pairs={{0,64},{64,0},{1,65},{65,1},{2,66},{66,2},{3,67},{67,3},{4,68},{68... | collective-permute-start | bytes 786440 | tf_op jit(solution)/shard_map/ppermute | solution.py:36
  217.5 6.3 %collective-permute-start.24 = (bf16[128,1024]{1,0:T(8,128)(2,1)S(1)}, bf16[128,1024]{1,0:T(8,128)(2,1)S(1)}, u32[]{:S(2)}, u32[]{:S(2)}) collective-permute-start(bf16[128,1024]{1,0:T(8,128)(2,1)S(1)} %collective-permute-done.23), channel_id=1, source_target_pairs={{0,64},{64,0},{1,65},{65,1},{2,66},{66,2},{3,67},{67,3},{4,68},{68... | collective-permute-start | bytes 786440 | tf_op jit(solution)/shard_map/ppermute | solution.py:36
  231.0 4.6 %all-to-all-start.5 = ((bf16[32,8,1024]{2,1,0:T(8,128)(2,1)}), bf16[32,8,1024]{2,1,0:T(8,128)(2,1)}, u32[]{:S(2)}, u32[]{:S(2)}) async-start(bf16[32,8,1024]{2,1,0:T(8,128)(2,1)} %bitcast.72), calls=%async_computation.5 | async-start | bytes 1048576 | tf_op jit(solution)/shard_map/all_to_all | solution.py:359
  235.6 14.0 %collective-permute-done.30 = bf16[1536,256]{1,0:T(8,128)(2,1)} collective-permute-done((bf16[1536,256]{1,0:T(8,128)(2,1)}, bf16[1536,256]{1,0:T(8,128)(2,1)}, u32[]{:S(2)}, u32[]{:S(2)}) %collective-permute-start.30) | collective-permute-done | bytes 786464 | tf_op jit(solution)/shard_map/ppermute | solution.py:36
  (145 shorter events, 47.3 us)
Async XLA Ops:
  2.6 17.2 %collective-permute-start.3 = (bf16[128,1152]{1,0:T(8,128)(2,1)}, bf16[128,1152]{1,0:T(8,128)(2,1)S(1)}, u32[]{:S(2)}, u32[]{:S(2)}) collective-permute-start(bf16[128,1152]{1,0:T(8,128)(2,1)} %get-tuple-element.45.refs_1_), channel_id=1, source_target_pairs={{0,7},{1,0},{2,1},{3,2},{4,3},{5,4},{6,5},{7,6},{8,15},{9,8},{10,9... | collective-permute-start | bytes 884744 | tf_op jit(solution)/shard_map/ppermute | solution.py:32
  9.0 13.9 %collective-permute-start.1 = (bf16[128,1152]{1,0:T(8,128)(2,1)}, bf16[128,1152]{1,0:T(8,128)(2,1)S(1)}, u32[]{:S(2)}, u32[]{:S(2)}) collective-permute-start(bf16[128,1152]{1,0:T(8,128)(2,1)} %get-tuple-element.45.refs_1_), channel_id=1, source_target_pairs={{0,1},{1,2},{2,3},{3,4},{4,5},{5,6},{6,7},{7,0},{8,9},{9,10},{10,1... | collective-permute-start | bytes 884744 | tf_op jit(solution)/shard_map/ppermute | solution.py:32
  9.0 13.9 %collective-permute-start.2 = (bf16[128,1024]{1,0:T(8,128)(2,1)}, bf16[128,1024]{1,0:T(8,128)(2,1)S(1)}, u32[]{:S(2)}, u32[]{:S(2)}) collective-permute-start(bf16[128,1024]{1,0:T(8,128)(2,1)} %get-tuple-element.44.refs_0_), channel_id=1, source_target_pairs={{0,7},{1,0},{2,1},{3,2},{4,3},{5,4},{6,5},{7,6},{8,15},{9,8},{10,9... | collective-permute-start | bytes 786440 | tf_op jit(solution)/shard_map/ppermute | solution.py:32
  11.7 13.9 %collective-permute-start = (bf16[128,1024]{1,0:T(8,128)(2,1)}, bf16[128,1024]{1,0:T(8,128)(2,1)S(1)}, u32[]{:S(2)}, u32[]{:S(2)}) collective-permute-start(bf16[128,1024]{1,0:T(8,128)(2,1)} %get-tuple-element.44.refs_0_), channel_id=1, source_target_pairs={{0,1},{1,2},{2,3},{3,4},{4,5},{5,6},{6,7},{7,0},{8,9},{9,10},{10,1... | collective-permute-start | bytes 786440 | tf_op jit(solution)/shard_map/ppermute | solution.py:32
  13.9 17.5 %all-to-all-start = ((bf16[8,128,256]{1,2,0:T(8,128)(2,1)}), bf16[8,128,256]{1,2,0:T(8,128)(2,1)S(1)}, u32[]{:S(2)}, u32[]{:S(2)}) async-start(bf16[8,128,256]{1,2,0:T(8,128)(2,1)} %bitcast.6), calls=%async_computation | async-start | bytes 1048576 | tf_op jit(solution)/shard_map/all_to_all | solution.py:295
  19.9 18.3 %collective-permute-start.7 = (bf16[128,1152]{1,0:T(8,128)(2,1)S(1)}, bf16[128,1152]{1,0:T(8,128)(2,1)S(1)}, u32[]{:S(2)}, u32[]{:S(2)}) collective-permute-start(bf16[128,1152]{1,0:T(8,128)(2,1)S(1)} %collective-permute-done.3.refs_5_), channel_id=1, source_target_pairs={{0,7},{1,0},{2,1},{3,2},{4,3},{5,4},{6,5},{7,6},{8,15},{9,8},{10,9... | collective-permute-start | bytes 884744 | tf_op jit(solution)/shard_map/ppermute | solution.py:32
  22.9 15.3 %collective-permute-start.5 = (bf16[128,1152]{1,0:T(8,128)(2,1)S(1)}, bf16[128,1152]{1,0:T(8,128)(2,1)S(1)}, u32[]{:S(2)}, u32[]{:S(2)}) collective-permute-start(bf16[128,1152]{1,0:T(8,128)(2,1)S(1)} %collective-permute-done.1.refs_3_), channel_id=1, source_target_pairs={{0,1},{1,2},{2,3},{3,4},{4,5},{5,6},{6,7},{7,0},{8,9},{9,10},{10,1... | collective-permute-start | bytes 884744 | tf_op jit(solution)/shard_map/ppermute | solution.py:32
  22.9 12.0 %collective-permute-start.6 = (bf16[128,1024]{1,0:T(8,128)(2,1)S(1)}, bf16[128,1024]{1,0:T(8,128)(2,1)S(1)}, u32[]{:S(2)}, u32[]{:S(2)}) collective-permute-start(bf16[128,1024]{1,0:T(8,128)(2,1)S(1)} %collective-permute-done.2.refs_4_), channel_id=1, source_target_pairs={{0,7},{1,0},{2,1},{3,2},{4,3},{5,4},{6,5},{7,6},{8,15},{9,8},{10,9... | collective-permute-start | bytes 786440 | tf_op jit(solution)/shard_map/ppermute | solution.py:32
  25.6 12.6 %collective-permute-start.4 = (bf16[128,1024]{1,0:T(8,128)(2,1)S(1)}, bf16[128,1024]{1,0:T(8,128)(2,1)}, u32[]{:S(2)}, u32[]{:S(2)}) collective-permute-start(bf16[128,1024]{1,0:T(8,128)(2,1)S(1)} %collective-permute-done.refs_2_), channel_id=1, source_target_pairs={{0,1},{1,2},{2,3},{3,4},{4,5},{5,6},{6,7},{7,0},{8,9},{9,10},{10,1... | collective-permute-start | bytes 786440 | tf_op jit(solution)/shard_map/ppermute | solution.py:32
  38.2 32.1 %all-to-all-start.1 = ((bf16[8,56,2048]{2,1,0:T(8,128)(2,1)}), bf16[8,56,2048]{2,1,0:T(8,128)(2,1)S(1)}, u32[]{:S(2)}, u32[]{:S(2)}) async-start(bf16[8,56,2048]{2,1,0:T(8,128)(2,1)} %get-tuple-element.48), calls=%async_computation.1 | async-start | bytes 3670016 | tf_op jit(solution)/shard_map/all_to_all | solution.py:308
  44.4 6.7 %collective-permute-start.9 = (bf16[128,1152]{1,0:T(8,128)(2,1)S(1)}, bf16[128,1152]{1,0:T(8,128)(2,1)S(1)}, u32[]{:S(2)}, u32[]{:S(2)}) collective-permute-start(bf16[128,1152]{1,0:T(8,128)(2,1)S(1)} %collective-permute-done.7.refs_3_), channel_id=1, source_target_pairs={{0,7},{1,0},{2,1},{3,2},{4,3},{5,4},{6,5},{7,6},{8,15},{9,8},{10,9... | collective-permute-start | bytes 884744 | tf_op jit(solution)/shard_map/ppermute | solution.py:32
  44.6 8.2 %collective-permute-start.10 = (bf16[128,1024]{1,0:T(8,128)(2,1)}, bf16[128,1024]{1,0:T(8,128)(2,1)S(1)}, u32[]{:S(2)}, u32[]{:S(2)}) collective-permute-start(bf16[128,1024]{1,0:T(8,128)(2,1)} %collective-permute-done.4.refs_0_), channel_id=1, source_target_pairs={{0,1},{1,2},{2,3},{3,4},{4,5},{5,6},{6,7},{7,0},{8,9},{9,10},{10,1... | collective-permute-start | bytes 786440 | tf_op jit(solution)/shard_map/ppermute | solution.py:32
  45.9 12.6 %collective-permute-start.11 = (bf16[128,1152]{1,0:T(8,128)(2,1)S(1)}, bf16[128,1152]{1,0:T(8,128)(2,1)S(1)}, u32[]{:S(2)}, u32[]{:S(2)}) collective-permute-start(bf16[128,1152]{1,0:T(8,128)(2,1)S(1)} %collective-permute-done.5.refs_1_), channel_id=1, source_target_pairs={{0,1},{1,2},{2,3},{3,4},{4,5},{5,6},{6,7},{7,0},{8,9},{9,10},{10,1... | collective-permute-start | bytes 884744 | tf_op jit(solution)/shard_map/ppermute | solution.py:32
  45.9 10.8 %collective-permute-start.8 = (bf16[128,1024]{1,0:T(8,128)(2,1)S(1)}, bf16[128,1024]{1,0:T(8,128)(2,1)S(1)}, u32[]{:S(2)}, u32[]{:S(2)}) collective-permute-start(bf16[128,1024]{1,0:T(8,128)(2,1)S(1)} %collective-permute-done.6.refs_2_), channel_id=1, source_target_pairs={{0,7},{1,0},{2,1},{3,2},{4,3},{5,4},{6,5},{7,6},{8,15},{9,8},{10,9... | collective-permute-start | bytes 786440 | tf_op jit(solution)/shard_map/ppermute | solution.py:32
  51.1 14.0 %collective-permute-start.13 = (bf16[128,1152]{1,0:T(8,128)(2,1)S(1)}, bf16[128,1152]{1,0:T(8,128)(2,1)S(1)}, u32[]{:S(2)}, u32[]{:S(2)}) collective-permute-start(bf16[128,1152]{1,0:T(8,128)(2,1)S(1)} %collective-permute-done.9.refs_7_.refs_1_), channel_id=1, source_target_pairs={{0,7},{1,0},{2,1},{3,2},{4,3},{5,4},{6,5},{7,6},{8,15},{9,8},{10,9... | collective-permute-start | bytes 884744 | tf_op jit(solution)/shard_map/ppermute | solution.py:32
  52.9 12.2 %collective-permute-start.12 = (bf16[128,1024]{1,0:T(8,128)(2,1)S(1)}, bf16[128,1024]{1,0:T(8,128)(2,1)S(1)}, u32[]{:S(2)}, u32[]{:S(2)}) collective-permute-start(bf16[128,1024]{1,0:T(8,128)(2,1)S(1)} %collective-permute-done.10.refs_4_), channel_id=1, source_target_pairs={{0,1},{1,2},{2,3},{3,4},{4,5},{5,6},{6,7},{7,0},{8,9},{9,10},{10,1... | collective-permute-start | bytes 786440 | tf_op jit(solution)/shard_map/ppermute | solution.py:32
  71.5 46.3 %all-to-all-start.2 = ((bf16[8,96,2048]{2,1,0:T(8,128)(2,1)}), bf16[8,96,2048]{2,1,0:T(8,128)(2,1)S(1)}, u32[]{:S(2)}, u32[]{:S(2)}) async-start(bf16[8,96,2048]{2,1,0:T(8,128)(2,1)} %get-tuple-element.60), calls=%async_computation.2 | async-start | bytes 6291456 | tf_op jit(solution)/shard_map/all_to_all | solution.py:308
  117.9 14.9 %all-to-all-start.3 = ((bf16[8,56,1024]{2,1,0:T(8,128)(2,1)}), bf16[8,56,1024]{2,1,0:T(8,128)(2,1)}, u32[]{:S(2)}, u32[]{:S(2)}) async-start(bf16[8,56,1024]{2,1,0:T(8,128)(2,1)} %bitcast.71), calls=%async_computation.3 | async-start | bytes 1835008 | tf_op jit(solution)/shard_map/all_to_all | solution.py:308
  132.8 28.2 %all-to-all-start.4 = ((bf16[8,96,1024]{2,1,0:T(8,128)(2,1)}), bf16[8,96,1024]{2,1,0:T(8,128)(2,1)S(1)}, u32[]{:S(2)}, u32[]{:S(2)}) async-start(bf16[8,96,1024]{2,1,0:T(8,128)(2,1)} %bitcast.70), calls=%async_computation.4 | async-start | bytes 3145728 | tf_op jit(solution)/shard_map/all_to_all | solution.py:308
  169.7 11.7 %collective-permute-start.15 = (bf16[128,1024]{1,0:T(8,128)(2,1)S(1)}, bf16[128,1024]{1,0:T(8,128)(2,1)S(1)}, u32[]{:S(2)}, u32[]{:S(2)}) collective-permute-start(bf16[128,1024]{1,0:T(8,128)(2,1)S(1)} %pad_maximum_fusion), channel_id=1, source_target_pairs={{0,1},{1,2},{2,3},{3,4},{4,5},{5,6},{6,7},{7,0},{8,9},{9,10},{10,1... | collective-permute-start | bytes 786440 | tf_op jit(solution)/shard_map/ppermute | solution.py:32
  169.8 14.9 %collective-permute-start.18 = (bf16[128,1024]{1,0:T(8,128)(2,1)S(1)}, bf16[128,1024]{1,0:T(8,128)(2,1)S(1)}, u32[]{:S(2)}, u32[]{:S(2)}) collective-permute-start(bf16[128,1024]{1,0:T(8,128)(2,1)S(1)} %pad_maximum_fusion.1), channel_id=1, source_target_pairs={{0,7},{1,0},{2,1},{3,2},{4,3},{5,4},{6,5},{7,6},{8,15},{9,8},{10,9... | collective-permute-start | bytes 786440 | tf_op jit(solution)/shard_map/ppermute | solution.py:32
  186.1 6.5 %collective-permute-start.19 = (bf16[128,1024]{1,0:T(8,128)(2,1)S(1)}, bf16[128,1024]{1,0:T(8,128)(2,1)S(1)}, u32[]{:S(2)}, u32[]{:S(2)}) collective-permute-start(bf16[128,1024]{1,0:T(8,128)(2,1)S(1)} %get-tuple-element.85), channel_id=1, source_target_pairs={{0,7},{1,0},{2,1},{3,2},{4,3},{5,4},{6,5},{7,6},{8,15},{9,8},{10,9... | collective-permute-start | bytes 786440 | tf_op jit(solution)/shard_map/ppermute | solution.py:32
  195.9 11.8 %collective-permute-start.20 = (bf16[128,1024]{1,0:T(8,128)(2,1)S(1)}, bf16[128,1024]{1,0:T(8,128)(2,1)S(1)}, u32[]{:S(2)}, u32[]{:S(2)}) collective-permute-start(bf16[128,1024]{1,0:T(8,128)(2,1)S(1)} %get-tuple-element.76), channel_id=1, source_target_pairs={{0,1},{1,2},{2,3},{3,4},{4,5},{5,6},{6,7},{7,0},{8,9},{9,10},{10,1... | collective-permute-start | bytes 786440 | tf_op jit(solution)/shard_map/ppermute | solution.py:32
  195.9 11.7 %collective-permute-start.21 = (bf16[128,1024]{1,0:T(8,128)(2,1)S(1)}, bf16[128,1024]{1,0:T(8,128)(2,1)S(1)}, u32[]{:S(2)}, u32[]{:S(2)}) collective-permute-start(bf16[128,1024]{1,0:T(8,128)(2,1)S(1)} %get-tuple-element.77), channel_id=1, source_target_pairs={{0,7},{1,0},{2,1},{3,2},{4,3},{5,4},{6,5},{7,6},{8,15},{9,8},{10,9... | collective-permute-start | bytes 786440 | tf_op jit(solution)/shard_map/ppermute | solution.py:32
  198.7 28.7 %collective-permute-start.29 = (bf16[2,1536,256]{2,1,0:T(8,128)(2,1)S(1)}, bf16[2,1536,256]{2,1,0:T(8,128)(2,1)S(1)}, u32[]{:S(2)}, u32[]{:S(2)}) collective-permute-start(bf16[2,1536,256]{2,1,0:T(8,128)(2,1)S(1)} %copy-done.16), channel_id=1, source_target_pairs={{0,64},{64,0},{1,65},{65,1},{2,66},{66,2},{3,67},{67,3},{4,68},{68... | collective-permute-start | bytes 4718600 | tf_op jit(solution)/shard_map/ppermute | solution.py:36
  208.2 9.3 %collective-permute-start.23 = (bf16[128,1024]{1,0:T(8,128)(2,1)S(1)}, bf16[128,1024]{1,0:T(8,128)(2,1)S(1)}, u32[]{:S(2)}, u32[]{:S(2)}) collective-permute-start(bf16[128,1024]{1,0:T(8,128)(2,1)S(1)} %get-tuple-element.84), channel_id=1, source_target_pairs={{0,128},{128,8},{8,136},{136,0},{1,129},{129,9},{9,137},{137,1},{2... | collective-permute-start | bytes 786440 | tf_op jit(solution)/shard_map/ppermute | solution.py:345
  208.6 15.3 %collective-permute-start.27 = (bf16[128,1024]{1,0:T(8,128)(2,1)S(1)}, bf16[128,1024]{1,0:T(8,128)(2,1)S(1)}, u32[]{:S(2)}, u32[]{:S(2)}) collective-permute-start(bf16[128,1024]{1,0:T(8,128)(2,1)S(1)} %get-tuple-element.84), channel_id=1, source_target_pairs={{0,8},{128,136},{8,0},{136,128},{1,9},{129,137},{9,1},{137,129},{2... | collective-permute-start | bytes 786440 | tf_op jit(solution)/shard_map/ppermute | solution.py:345
  210.6 13.4 %collective-permute-start.25 = (bf16[128,1024]{1,0:T(8,128)(2,1)S(1)}, bf16[128,1024]{1,0:T(8,128)(2,1)S(1)}, u32[]{:S(2)}, u32[]{:S(2)}) collective-permute-start(bf16[128,1024]{1,0:T(8,128)(2,1)S(1)} %get-tuple-element.84), channel_id=1, source_target_pairs={{0,136},{128,0},{8,128},{136,8},{1,137},{129,1},{9,129},{137,9},{2... | collective-permute-start | bytes 786440 | tf_op jit(solution)/shard_map/ppermute | solution.py:345
  211.8 12.8 %collective-permute-start.22 = (bf16[128,1024]{1,0:T(8,128)(2,1)S(1)}, bf16[128,1024]{1,0:T(8,128)(2,1)S(1)}, u32[]{:S(2)}, u32[]{:S(2)}) collective-permute-start(bf16[128,1024]{1,0:T(8,128)(2,1)S(1)} %get-tuple-element.84), channel_id=1, source_target_pairs={{0,64},{64,0},{1,65},{65,1},{2,66},{66,2},{3,67},{67,3},{4,68},{68... | collective-permute-start | bytes 786440 | tf_op jit(solution)/shard_map/ppermute | solution.py:36
  217.5 7.4 %collective-permute-start.24 = (bf16[128,1024]{1,0:T(8,128)(2,1)S(1)}, bf16[128,1024]{1,0:T(8,128)(2,1)S(1)}, u32[]{:S(2)}, u32[]{:S(2)}) collective-permute-start(bf16[128,1024]{1,0:T(8,128)(2,1)S(1)} %collective-permute-done.23), channel_id=1, source_target_pairs={{0,64},{64,0},{1,65},{65,1},{2,66},{66,2},{3,67},{67,3},{4,68},{68... | collective-permute-start | bytes 786440 | tf_op jit(solution)/shard_map/ppermute | solution.py:36
  230.4 19.2 %collective-permute-start.30 = (bf16[1536,256]{1,0:T(8,128)(2,1)}, bf16[1536,256]{1,0:T(8,128)(2,1)}, u32[]{:S(2)}, u32[]{:S(2)}) collective-permute-start(bf16[1536,256]{1,0:T(8,128)(2,1)} %fusion.10), channel_id=1, source_target_pairs={{0,128},{128,0},{1,129},{129,1},{2,130},{130,2},{3,131},{131,3},{4... | collective-permute-start | bytes 2359304 | tf_op jit(solution)/shard_map/ppermute | solution.py:36
  231.0 22.4 %all-to-all-start.5 = ((bf16[32,8,1024]{2,1,0:T(8,128)(2,1)}), bf16[32,8,1024]{2,1,0:T(8,128)(2,1)}, u32[]{:S(2)}, u32[]{:S(2)}) async-start(bf16[32,8,1024]{2,1,0:T(8,128)(2,1)} %bitcast.72), calls=%async_computation.5 | async-start | bytes 1048576 | tf_op jit(solution)/shard_map/all_to_all | solution.py:359
  (32 other events, 282.5 us)
